TPU v7x, 32 devices: a whole 2x2x4 slice. The times are simulated.
32 devices in a mesh: sec: 2 (over y), dev: 16 (over z, x, core).
Axes of the slice: x: 2, y: 2, z: 4, core: 2. Of those that a mesh axis runs over, the one named last changes fastest.
Arguments:
- sources: float32 [2, 8, 8192], P(None, None, ('sec', 'dev')), may hold values from -16 to 16
- positions: float32 [3, 8192], P(None, ('sec', 'dev')), may hold values from -0.5 to 16, as said below
- weights: float32 [8192], P(('sec', 'dev')), may hold values from 0.5 to 2
- wavenumbers: float32 [8], replicated, may hold values from 1 to 8
- directions: float32 [3, 128], replicated, may hold values from -1 to 1
- box_centers: float32 [3, 32], replicated, may hold values from -0.25 to 16
- group_centers: float32 [3, 4], replicated, may hold values from -0.25 to 16
- near_pairs: int32 [32, 2, 10], P(('sec', 'dev')), may hold values from 0 to 5, as said below
- pair_counts: int32 [32], P(('sec', 'dev')), may hold values from 3 to 10, as said below
- box_lists: int32 [32, 4], P(('sec', 'dev')), may hold values from 0 to 31, as said below
- group_lists: int32 [4, 2], replicated, may hold values from 0 to 3, as said below
Outputs:
- result: float32 [2, 8, 8192], P(None, None, ('sec', 'dev'))
- rayleigh: float32 [2, 8], replicated
Inputs may be any that keep to these rules, and one draw needn't show every extreme that they name: `positions`: panels of leaf l lie within half a unit of a grid point of a 16 by 16 layered grid, leaves in order along it. `near_pairs`: row 0 holds leaves of the device's own box, row 1 leaves of its window; the first three pairs of every device take a source leaf of the box before, of the box after, and the target leaf itself. `pair_counts`: some device has all 10 pairs live. `box_lists`: A row holds distinct boxes, never the box itself or the ones just before and after it. `group_lists`: A row holds distinct groups other than the group itself.
All inputs are finite; a program needn't handle non-finite values.
Results may differ from a plain program's by a relative error of at most 0.0003.
Values sent between devices are 32-bit elements; how exact they have to be, the bound alone decides.
A program may use at most 64 MiB of HBM per device.

v0:
```python
import math

import jax
import jax.numpy as jnp
from jax import lax
from jax.sharding import PartitionSpec as P

LEAF = 128
LEAVES = 2
F = 8
Q = 128
PAIRS_LEAF = 5
ML1 = 4
ML2 = 2
GROUP = 8
P_DEV = 256
PAIRS_MAX = 10


SOFT = 0.1


def with_halo(cells, sides, width):
    for axis, dim in sides:
        count = lax.axis_size(axis)
        ends = count - 1
        head = lax.slice_in_dim(cells, 0, width, axis=dim)
        tail = lax.slice_in_dim(cells, cells.shape[dim] - width, cells.shape[dim], axis=dim)
        cells = jnp.concatenate(
            [
                lax.ppermute(tail, axis, [(i, (i + 1) % count) for i in range(ends)]),
                cells,
                lax.ppermute(head, axis, [((i + 1) % count, i) for i in range(ends)]),
            ],
            axis=dim,
        )
    return cells


def kernel_block(targets_xyz, sources_xyz, wave_numbers, reach_scale):
    offsets = targets_xyz[:, :, None] - sources_xyz[:, None, :]
    distance = jnp.sqrt(jnp.sum(offsets * offsets, axis=0) + SOFT * SOFT)
    amplitude = reach_scale / distance
    phases = wave_numbers[:, None, None] * distance[None, :, :]
    return (amplitude[None] * jnp.cos(phases), amplitude[None] * jnp.sin(phases))


def apply_block(kernel, values):
    real_kernel, imag_kernel = kernel
    highest = lax.Precision.HIGHEST
    real_real = jnp.einsum("fab,fb->fa", real_kernel, values[0], precision=highest)
    imag_imag = jnp.einsum("fab,fb->fa", imag_kernel, values[1], precision=highest)
    real_imag = jnp.einsum("fab,fb->fa", real_kernel, values[1], precision=highest)
    imag_real = jnp.einsum("fab,fb->fa", imag_kernel, values[0], precision=highest)
    return jnp.stack([real_real - imag_imag, real_imag + imag_real])


def apply_transposed(kernel, values):
    real_kernel, imag_kernel = kernel
    highest = lax.Precision.HIGHEST
    real_real = jnp.einsum("fba,fb->fa", real_kernel, values[0], precision=highest)
    imag_imag = jnp.einsum("fba,fb->fa", imag_kernel, values[1], precision=highest)
    real_imag = jnp.einsum("fba,fb->fa", real_kernel, values[1], precision=highest)
    imag_real = jnp.einsum("fba,fb->fa", imag_kernel, values[0], precision=highest)
    return jnp.stack([real_real - imag_imag, real_imag + imag_real])


def on_device(
    sources,
    positions,
    weights,
    wavenumbers,
    directions,
    box_centers,
    group_centers,
    near_pairs,
    pair_counts,
    box_lists,
    group_lists,
):
    radius_box = 1.0 + 0.5 * LEAVES
    radius_group = 2.0 * radius_box
    device_index = lax.axis_index(("sec", "dev"))
    weighted = sources * weights[None, None, :]
    packed = jnp.concatenate([weighted.reshape(2 * F, P_DEV), positions], axis=0)
    window = with_halo(packed, ((("sec", "dev"), 1),), P_DEV)
    window_values = window[: 2 * F].reshape(2, F, 3 * LEAVES, LEAF)
    window_xyz = window[2 * F :].reshape(3, 3 * LEAVES, LEAF)
    local_xyz = positions.reshape(3, LEAVES, LEAF)
    targets = near_pairs[0, 0]
    anchors = near_pairs[0, 1]
    live_count = pair_counts[0]
    pair_block = math.gcd(8, PAIRS_MAX)
    leaf_ids = jnp.arange(LEAVES, dtype=jnp.int32)
    pair_ids = jnp.arange(pair_block, dtype=jnp.int32)
    batched_kernel = jax.vmap(kernel_block, in_axes=(1, 1, None, None))
    batched_apply = jax.vmap(apply_block, in_axes=(0, 2), out_axes=2)

    def near_turn(turn_index, near_total):
        first_pair = turn_index * pair_block
        target_ids = lax.dynamic_slice_in_dim(targets, first_pair, pair_block)
        anchor_ids = lax.dynamic_slice_in_dim(anchors, first_pair, pair_block)
        kernels = batched_kernel(
            local_xyz[:, target_ids], window_xyz[:, anchor_ids], wavenumbers, 1.0
        )
        blocks = batched_apply(kernels, window_values[:, :, anchor_ids])
        live_rows = first_pair + pair_ids < live_count
        placing = ((target_ids[:, None] == leaf_ids[None, :]) & live_rows[:, None]).astype(
            jnp.float32
        )
        return near_total + jnp.einsum(
            "rfsa,sl->rfla", blocks, placing, precision=lax.Precision.HIGHEST
        )

    turn_count = (live_count + pair_block - 1) // pair_block
    near_total = lax.fori_loop(
        0, turn_count, near_turn, jnp.zeros((2, F, LEAVES, LEAF), jnp.float32)
    )
    near_total = near_total.reshape(2, F, P_DEV)
    own_center = lax.dynamic_index_in_dim(box_centers, device_index, 1, keepdims=False)
    own_proxies = own_center[:, None] + radius_box * directions
    outward = kernel_block(own_proxies, positions, wavenumbers, radius_box)
    own_multipole = apply_block(outward, weighted) / math.sqrt(P_DEV)
    parent = device_index // GROUP
    parent_proxies = (
        lax.dynamic_index_in_dim(group_centers, parent, 1, keepdims=False)[:, None]
        + radius_group * directions
    )
    source_groups = lax.dynamic_index_in_dim(group_lists, parent, 0, keepdims=False)
    contribution = apply_block(
        kernel_block(parent_proxies, own_proxies, wavenumbers, radius_group), own_multipole
    ) / math.sqrt(GROUP * Q)
    gathered, contributions = (
        lax.all_gather(own_multipole[None], ("sec", "dev"), axis=0, tiled=True),
        lax.all_gather(contribution[None], ("sec", "dev"), axis=0, tiled=True),
    )
    group_count = contributions.shape[0] // GROUP
    group_multipoles = contributions.reshape(group_count, GROUP, 2, F, Q).sum(1)
    source_multipoles = group_multipoles[source_groups]
    source_boxes = box_lists[0]
    source_proxies = box_centers[:, source_boxes][:, :, None] + radius_box * directions[:, None, :]
    kernels = jax.vmap(kernel_block, in_axes=(None, 1, None, None))(
        own_proxies, source_proxies, wavenumbers, radius_box
    )
    incoming = jax.vmap(apply_block)(kernels, gathered[source_boxes]).sum(0) / math.sqrt(ML1 * Q)
    group_proxies = (
        group_centers[:, source_groups][:, :, None] + radius_group * directions[:, None, :]
    )
    group_kernels = jax.vmap(kernel_block, in_axes=(None, 1, None, None))(
        parent_proxies, group_proxies, wavenumbers, radius_group
    )
    group_local = jax.vmap(apply_block)(group_kernels, source_multipoles).sum(0) / math.sqrt(
        ML2 * Q
    )
    descended = apply_block(
        kernel_block(own_proxies, parent_proxies, wavenumbers, radius_group), group_local
    ) / math.sqrt(Q)
    box_local = incoming + descended
    far_field = apply_transposed(outward, box_local) / math.sqrt(Q)
    result = 0.5 * sources + near_total / math.sqrt(LEAF * PAIRS_LEAF) + far_field
    real_sum = jnp.sum(sources[0] * result[0] + sources[1] * result[1], axis=-1)
    imag_sum = jnp.sum(sources[0] * result[1] - sources[1] * result[0], axis=-1)
    squares = jnp.sum(sources[0] * sources[0] + sources[1] * sources[1], axis=-1)
    numerator, denominator = lax.psum((jnp.stack([real_sum, imag_sum]), squares), ("sec", "dev"))
    rayleigh = numerator / (denominator + 1e-06)[None, :]
    return (result, rayleigh)


def solution(mesh):
    in_specs = (
        P(None, None, ("sec", "dev")),
        P(None, ("sec", "dev")),
        P(("sec", "dev")),
        P(),
        P(),
        P(),
        P(),
        P(("sec", "dev"), None, None),
        P(("sec", "dev")),
        P(("sec", "dev"), None),
        P(),
    )
    out_specs = (P(None, None, ("sec", "dev")), P())
    return jax.shard_map(
        on_device, mesh=mesh, in_specs=in_specs, out_specs=out_specs, check_vma=False
    )
```

profile of v0, /device:TPU:0, one launch (start us, length us, event | category | flops | bytes accessed | tf_op | source)
XLA Modules:
  0.0 386.1 jit_solution(563633886877796727)
XLA Ops:
  18.6 4.7 %fusion.52 = f32[8,1,128]{2,1,0:T(1,128)S(1)} fusion(f32[128,256]{1,0:T(8,128)S(1)} %get-tuple-element.212, f32[8]{0:T(128)S(1)} %copy-done.8, f32[128,256]{1,0:T(8,128)S(1)} %get-tuple-element.211, f32[8,256,1]{1,0,2:T(8,128)S(1)} %get-tuple-element.222), kind=kOutput, calls=%fused_computation.68 | convolution fusion | flops 3670016 | bytes 274464 | tf_op jit(solution)/shard_map/fab,fb->fa/dot_general | solution.py:53
  23.3 4.5 %fusion.63 = f32[8,1,128]{2,1,0:T(1,128)S(1)} fusion(f32[128,256]{1,0:T(8,128)S(1)} %get-tuple-element.212, f32[8]{0:T(128)S(1)} %copy-done.8, f32[128,256]{1,0:T(8,128)S(1)} %get-tuple-element.211, f32[8,256,1]{1,0,2:T(8,128)S(1)} %get-tuple-element.222), kind=kOutput, calls=%fused_computation.74 | convolution fusion | flops 3670016 | bytes 274464 | tf_op jit(solution)/shard_map/fab,fb->fa/dot_general | solution.py:52
  33.3 13.3 %fusion.98 = f32[8,1,128]{2,1,0:T(1,128)S(1)} fusion(f32[8,128,1]{1,2,0:T(1,128)S(1)} %bitcast.280, f32[128,128]{1,0:T(8,128)S(1)} %get-tuple-element.216, f32[128,128]{1,0:T(8,128)S(1)} %get-tuple-element.215, f32[8]{0:T(128)S(1)} %copy-done.8), kind=kOutput, calls=%fused_computation.105 | convolution fusion | flops 1835008 | bytes 139296 | tf_op jit(solution)/shard_map/fab,fb->fa/dot_general | solution.py:53
  49.4 43.9 %all_gather.7 = f32[32,2,8,128]{3,2,1,0:T(8,128)S(1)} all-gather(f32[1,2,8,128]{3,2,1,0:T(8,128)S(1)} %maximum_multiply_fusion.3), channel_id=1, replica_groups=mesh['sec'=2,'dev'=16] {'sec','dev'}, dimensions={0}, use_global_device_ids=true | all-gather | bytes 270336 | tf_op jit(solution)/shard_map/all_gather | solution.py:135
  95.0 5.1 %fusion.71 = f32[2,8,1,128]{3,2,1,0:T(1,128)S(1)} fusion(f32[2,8,128,1]{2,3,1,0:T(1,128)S(1)} %bitcast.270, f32[2,128,128]{2,1,0:T(8,128)S(1)} %get-tuple-element.210, f32[8]{0:T(128)S(1)} %copy-done.8, f32[2,128,128]{2,1,0:T(8,128)S(1)} %get-tuple-element.209), kind=kOutput, calls=%fused_computation.79 | convolution fusion | flops 3670016 | bytes 278560 | tf_op jit(solution)/shard_map/vmap(fab,fb->fa)/dot_general | solution.py:54
  100.1 5.1 %fusion.68 = f32[2,8,1,128]{3,2,1,0:T(1,128)S(1)} fusion(f32[2,8,128,1]{2,3,1,0:T(1,128)S(1)} %bitcast.271, f32[2,128,128]{2,1,0:T(8,128)S(1)} %get-tuple-element.210, f32[8]{0:T(128)S(1)} %copy-done.8, f32[2,128,128]{2,1,0:T(8,128)S(1)} %get-tuple-element.209), kind=kOutput, calls=%fused_computation.77 | convolution fusion | flops 3670016 | bytes 278560 | tf_op jit(solution)/shard_map/vmap(fab,fb->fa)/dot_general | solution.py:51
  105.2 5.5 %fusion.66 = f32[2,8,1,128]{3,2,1,0:T(1,128)S(1)} fusion(f32[2,8,128,1]{2,3,1,0:T(1,128)S(1)} %bitcast.268, f32[2,128,128]{2,1,0:T(8,128)S(1)} %get-tuple-element.210, f32[8]{0:T(128)S(1)} %copy-done.8, f32[2,128,128]{2,1,0:T(8,128)S(1)} %get-tuple-element.209), kind=kOutput, calls=%fused_computation.76 | convolution fusion | flops 3670016 | bytes 278560 | tf_op jit(solution)/shard_map/vmap(fab,fb->fa)/dot_general | solution.py:53
  110.7 5.1 %fusion.73 = f32[2,8,1,128]{3,2,1,0:T(1,128)S(1)} fusion(f32[2,8,128,1]{2,3,1,0:T(1,128)S(1)} %bitcast.269, f32[2,128,128]{2,1,0:T(8,128)S(1)} %get-tuple-element.210, f32[8]{0:T(128)S(1)} %copy-done.8, f32[2,128,128]{2,1,0:T(8,128)S(1)} %get-tuple-element.209), kind=kOutput, calls=%fused_computation.80 | convolution fusion | flops 3670016 | bytes 278560 | tf_op jit(solution)/shard_map/vmap(fab,fb->fa)/dot_general | solution.py:52
  126.9 37.3 %all_gather.6 = f32[32,2,8,128]{3,2,1,0:T(8,128)S(1)} all-gather(f32[1,2,8,128]{3,2,1,0:T(8,128)S(1)} %maximum_multiply_fusion.1), channel_id=1, replica_groups=mesh['sec'=2,'dev'=16] {'sec','dev'}, dimensions={0}, use_global_device_ids=true | all-gather | bytes 270336 | tf_op jit(solution)/shard_map/all_gather | solution.py:134
  165.7 10.1 %fusion.43 = f32[4,8,1,128]{3,2,1,0:T(1,128)S(1)} fusion(f32[4,8,128,1]{2,3,1,0:T(1,128)S(1)} %bitcast.262, f32[4,128,128]{2,1,0:T(8,128)S(1)} %get-tuple-element.208, f32[8]{0:T(128)S(1)} %copy-done.8, f32[4,128,128]{2,1,0:T(8,128)S(1)} %get-tuple-element.207), kind=kOutput, calls=%fused_computation.59 | convolution fusion | flops 7340032 | bytes 557088 | tf_op jit(solution)/shard_map/vmap(fab,fb->fa)/dot_general | solution.py:54
  175.8 10.4 %fusion.40 = f32[4,8,1,128]{3,2,1,0:T(1,128)S(1)} fusion(f32[4,8,128,1]{2,3,1,0:T(1,128)S(1)} %bitcast.263, f32[4,128,128]{2,1,0:T(8,128)S(1)} %get-tuple-element.208, f32[8]{0:T(128)S(1)} %copy-done.8, f32[4,128,128]{2,1,0:T(8,128)S(1)} %get-tuple-element.207), kind=kOutput, calls=%fused_computation.57 | convolution fusion | flops 7340032 | bytes 557088 | tf_op jit(solution)/shard_map/vmap(fab,fb->fa)/dot_general | solution.py:51
  186.2 10.2 %fusion.38 = f32[4,8,1,128]{3,2,1,0:T(1,128)S(1)} fusion(f32[4,8,128,1]{2,3,1,0:T(1,128)S(1)} %bitcast.260, f32[4,128,128]{2,1,0:T(8,128)S(1)} %get-tuple-element.208, f32[8]{0:T(128)S(1)} %copy-done.8, f32[4,128,128]{2,1,0:T(8,128)S(1)} %get-tuple-element.207), kind=kOutput, calls=%fused_computation.56 | convolution fusion | flops 7340032 | bytes 557088 | tf_op jit(solution)/shard_map/vmap(fab,fb->fa)/dot_general | solution.py:53
  196.4 10.3 %fusion.45 = f32[4,8,1,128]{3,2,1,0:T(1,128)S(1)} fusion(f32[4,8,128,1]{2,3,1,0:T(1,128)S(1)} %bitcast.261, f32[4,128,128]{2,1,0:T(8,128)S(1)} %get-tuple-element.208, f32[8]{0:T(128)S(1)} %copy-done.8, f32[4,128,128]{2,1,0:T(8,128)S(1)} %get-tuple-element.207), kind=kOutput, calls=%fused_computation.60 | convolution fusion | flops 7340032 | bytes 557088 | tf_op jit(solution)/shard_map/vmap(fab,fb->fa)/dot_general | solution.py:52
  215.0 4.6 %fusion.57 = f32[8,1,256]{2,1,0:T(1,128)S(1)} fusion(f32[8,128,1]{1,2,0:T(1,128)S(1)} %bitcast.291, f32[128,256]{1,0:T(8,128)S(1)} %get-tuple-element.212, f32[8]{0:T(128)S(1)} %copy-done.8, f32[128,256]{1,0:T(8,128)S(1)} %get-tuple-element.211), kind=kOutput, calls=%fused_computation.71 | convolution fusion | flops 3670016 | bytes 274464 | tf_op jit(solution)/shard_map/fba,fb->fa/dot_general | solution.py:64
  224.5 53.2 %while.13 = (s32[]{:T(128)}, f32[2,8,2,128]{3,2,1,0:T(2,128)S(1)}, s32[]{:T(128)}, s32[10]{0:T(128)S(1)}, s32[]{:T(128)}, /*index=5*/f32[3,2,128]{2,0,1:T(4,128)...) while((s32[]{:T(128)}, f32[2,8,2,128]{3,2,1,0:T(2,128)S(1)}, ...), condition=%wide.region_2.3_spmd.clone.clone, body=%wide.region_0.2_spmd.clone.clone.sunk | while | flops 15087646 | bytes 1829283 | solution.py:116
  232.7 5.1 %fusion.237 = f32[2,8,1,128]{3,2,1,0:T(1,128)S(1)} fusion(f32[2,8,128,1]{2,3,1,0:T(1,128)S(1)} %bitcast.252, f32[2,128,128]{2,1,0:T(8,128)S(1)} %get-tuple-element.313, f32[8]{0:T(128)S(1)} %get-tuple-element.353, f32[2,128,128]{2,1,0:T(8,128)S(1)} %get-tuple-element.314), kind=kOutput, calls=%fused_computation.16.clone.1 | convolution fusion | flops 3670016 | bytes 278560 | tf_op jit(solution)/shard_map/while/body/vmap(fab,fb->fa)/dot_general | solution.py:54
  237.8 5.1 %fusion.238 = f32[2,8,1,128]{3,2,1,0:T(1,128)S(1)} fusion(f32[2,8,128,1]{2,3,1,0:T(1,128)S(1)} %bitcast.254, f32[2,128,128]{2,1,0:T(8,128)S(1)} %get-tuple-element.313, f32[8]{0:T(128)S(1)} %get-tuple-element.353, f32[2,128,128]{2,1,0:T(8,128)S(1)} %get-tuple-element.314), kind=kOutput, calls=%fused_computation.13.clone.1 | convolution fusion | flops 3670016 | bytes 278560 | tf_op jit(solution)/shard_map/while/body/vmap(fab,fb->fa)/dot_general | solution.py:53
  243.0 5.1 %fusion.240 = f32[2,8,1,128]{3,2,1,0:T(1,128)S(1)} fusion(f32[2,8,128,1]{2,3,1,0:T(1,128)S(1)} %bitcast.255, f32[2,128,128]{2,1,0:T(8,128)S(1)} %get-tuple-element.313, f32[8]{0:T(128)S(1)} %get-tuple-element.353, f32[2,128,128]{2,1,0:T(8,128)S(1)} %get-tuple-element.314), kind=kOutput, calls=%fused_computation.17.clone.1 | convolution fusion | flops 3670016 | bytes 278560 | tf_op jit(solution)/shard_map/while/body/vmap(fab,fb->fa)/dot_general | solution.py:52
  248.1 5.1 %fusion.241 = f32[2,8,1,128]{3,2,1,0:T(1,128)S(1)} fusion(f32[2,8,128,1]{2,3,1,0:T(1,128)S(1)} %bitcast.253, f32[2,128,128]{2,1,0:T(8,128)S(1)} %get-tuple-element.313, f32[8]{0:T(128)S(1)} %get-tuple-element.353, f32[2,128,128]{2,1,0:T(8,128)S(1)} %get-tuple-element.314), kind=kOutput, calls=%fused_computation.14.clone.1 | convolution fusion | flops 3670016 | bytes 278560 | tf_op jit(solution)/shard_map/while/body/vmap(fab,fb->fa)/dot_general | solution.py:51
  256.1 5.1 %fusion.237 = f32[2,8,1,128]{3,2,1,0:T(1,128)S(1)} fusion(f32[2,8,128,1]{2,3,1,0:T(1,128)S(1)} %bitcast.252, f32[2,128,128]{2,1,0:T(8,128)S(1)} %get-tuple-element.313, f32[8]{0:T(128)S(1)} %get-tuple-element.353, f32[2,128,128]{2,1,0:T(8,128)S(1)} %get-tuple-element.314), kind=kOutput, calls=%fused_computation.16.clone.1 | convolution fusion | flops 3670016 | bytes 278560 | tf_op jit(solution)/shard_map/while/body/vmap(fab,fb->fa)/dot_general | solution.py:54
  261.2 5.1 %fusion.238 = f32[2,8,1,128]{3,2,1,0:T(1,128)S(1)} fusion(f32[2,8,128,1]{2,3,1,0:T(1,128)S(1)} %bitcast.254, f32[2,128,128]{2,1,0:T(8,128)S(1)} %get-tuple-element.313, f32[8]{0:T(128)S(1)} %get-tuple-element.353, f32[2,128,128]{2,1,0:T(8,128)S(1)} %get-tuple-element.314), kind=kOutput, calls=%fused_computation.13.clone.1 | convolution fusion | flops 3670016 | bytes 278560 | tf_op jit(solution)/shard_map/while/body/vmap(fab,fb->fa)/dot_general | solution.py:53
  266.4 5.1 %fusion.240 = f32[2,8,1,128]{3,2,1,0:T(1,128)S(1)} fusion(f32[2,8,128,1]{2,3,1,0:T(1,128)S(1)} %bitcast.255, f32[2,128,128]{2,1,0:T(8,128)S(1)} %get-tuple-element.313, f32[8]{0:T(128)S(1)} %get-tuple-element.353, f32[2,128,128]{2,1,0:T(8,128)S(1)} %get-tuple-element.314), kind=kOutput, calls=%fused_computation.17.clone.1 | convolution fusion | flops 3670016 | bytes 278560 | tf_op jit(solution)/shard_map/while/body/vmap(fab,fb->fa)/dot_general | solution.py:52
  271.5 5.1 %fusion.241 = f32[2,8,1,128]{3,2,1,0:T(1,128)S(1)} fusion(f32[2,8,128,1]{2,3,1,0:T(1,128)S(1)} %bitcast.253, f32[2,128,128]{2,1,0:T(8,128)S(1)} %get-tuple-element.313, f32[8]{0:T(128)S(1)} %get-tuple-element.353, f32[2,128,128]{2,1,0:T(8,128)S(1)} %get-tuple-element.314), kind=kOutput, calls=%fused_computation.14.clone.1 | convolution fusion | flops 3670016 | bytes 278560 | tf_op jit(solution)/shard_map/while/body/vmap(fab,fb->fa)/dot_general | solution.py:51
  278.0 107.3 %all-reduce = (f32[2,8]{1,0:T(2,128)S(1)}, f32[8]{0:T(128)S(1)}) all-reduce(f32[2,8]{1,0:T(2,128)S(1)} %pad_maximum_fusion.4, f32[8]{0:T(128)S(1)} %get-tuple-element.175), channel_id=1, replica_groups=mesh['sec'=2,'dev'=16] {'sec','dev'}, use_global_device_ids=true, to_apply=%region_13.14 | all-reduce | flops 24 | bytes 192 | tf_op jit(solution)/shard_map/psum | solution.py:164
  (124 shorter events, 59.2 us)
Async XLA Ops:
  0.6 92.8 %copy-start = (s32[4,2]{0,1:T(2,128)S(1)}, s32[4,2]{0,1:T(2,128)}, u32[]{:S(2)}) copy-start(s32[4,2]{0,1:T(2,128)} %param.23) | copy-start | bytes 100
  2.1 222.4 %collective-permute-start.1 = (f32[19,256]{1,0:T(8,128)S(1)}, f32[19,256]{1,0:T(8,128)S(1)}, u32[]{:S(2)}, u32[]{:S(2)}) collective-permute-start(f32[19,256]{1,0:T(8,128)S(1)} %pad_maximum_fusion.3), channel_id=1, source_target_pairs={{1,0},{2,1},{3,2},{4,3},{5,4},{6,5},{7,6},{8,7},{9,8},{10,9},{11,1... | collective-permute-start | bytes 58376 | tf_op jit(solution)/shard_map/ppermute | solution.py:33
  3.4 221.1 %collective-permute-start = (f32[19,256]{1,0:T(8,128)S(1)}, f32[19,256]{1,0:T(8,128)S(1)}, u32[]{:S(2)}, u32[]{:S(2)}) collective-permute-start(f32[19,256]{1,0:T(8,128)S(1)} %pad_maximum_fusion.3), channel_id=1, source_target_pairs={{0,1},{1,2},{2,3},{3,4},{4,5},{5,6},{6,7},{7,8},{8,9},{9,10},{10,1... | collective-permute-start | bytes 58376 | tf_op jit(solution)/shard_map/ppermute | solution.py:31
  8.8 0.9 copy-start.8
  46.6 2.7 copy-start.5
  124.1 2.7 copy-start.4
  126.8 37.4 %copy-start.7 = (s32[1,4]{1,0:T(1,128)S(1)}, s32[1,4]{1,0:T(1,128)}, u32[]{:S(2)}) copy-start(s32[1,4]{1,0:T(1,128)} %param.22) | copy-start | bytes 52
  219.6 4.1 %copy-start.6 = (s32[1,2,10]{2,1,0:T(2,128)S(1)}, s32[1,2,10]{2,1,0:T(2,128)}, u32[]{:S(2)}) copy-start(s32[1,2,10]{2,1,0:T(2,128)} %param.20) | copy-start | bytes 244
  219.6 4.8 %copy-start.2 = (f32[3,256]{1,0:T(4,128)S(1)}, f32[3,256]{1,0:T(4,128)}, u32[]{:S(2)}) copy-start(f32[3,256]{1,0:T(4,128)} %param.14) | copy-start | bytes 9220
  224.5 53.2 %copy-start.1 = (f32[2,8,256]{2,1,0:T(8,128)S(1)}, f32[2,8,256]{2,1,0:T(8,128)}, u32[]{:S(2)}) copy-start(f32[2,8,256]{2,1,0:T(8,128)} %param.13) | copy-start | bytes 49156
  277.8 108.1 %copy-start.3 = (f32[2,8,256]{2,1,0:T(8,128)}, f32[2,8,256]{2,1,0:T(8,128)S(1)}, u32[]{:S(2)}) copy-start(f32[2,8,256]{2,1,0:T(8,128)S(1)} %fusion.168) | copy-start | bytes 49156
where the time goes:
time: 390 us; the launch traced here: 386 us
  blocking collectives  189 us (48%)
  matrix products  170 us (44%)
  other arithmetic  7.43 us (2%)
  local copies, waits for them, and re-layouts  6.98 us (2%)
  loops' own time  6.52 us (2%)
  starting transfers between devices  4.31 us (1%)
    psum x1, blocking collectives, on_device(): lax.psum((jnp.stack([real_sum, imag_sum]), squares), ('sec', 'dev'))  107 us
    dot_general x7, matrix products, apply_block(): jnp.einsum('fab,fb->fa', real_kernel, values[1], precision=highest)  46.7 us
    all_gather x1, blocking collectives, on_device(): lax.all_gather(contribution[None], ('sec', 'dev'), axis=0, tiled=True)  43.9 us
    all_gather x1, blocking collectives, on_device(): lax.all_gather(own_multipole[None], ('sec', 'dev'), axis=0, tiled=True)  37.3 us
    dot_general x7, matrix products, apply_block(): jnp.einsum('fab,fb->fa', real_kernel, values[0], precision=highest)  35.5 us
    dot_general x7, matrix products, apply_block(): jnp.einsum('fab,fb->fa', imag_kernel, values[1], precision=highest)  35.5 us
    dot_general x7, matrix products, apply_block(): jnp.einsum('fab,fb->fa', imag_kernel, values[0], precision=highest)  35.2 us
  transfers between devices with their start and end apart: 2, of which 0 were waited for; matrix products, arithmetic and copies ran while one was open for 35% of the time, Pallas kernels for 0%

commit v1 on v0

v1 whole, which is shorter than its diff:
```python
import functools
import math

import jax
import jax.numpy as jnp
from jax import lax
from jax.experimental import pallas as pl
from jax.experimental.pallas import tpu as pltpu
from jax.sharding import PartitionSpec as P

LEAF = 128
LEAVES = 2
F = 8
Q = 128
PAIRS_LEAF = 5
ML1 = 4
ML2 = 2
GROUP = 8
P_DEV = 256
PAIRS_MAX = 10

SOFT = 0.1
RADIUS_BOX = 1.0 + 0.5 * LEAVES
RADIUS_GROUP = 2.0 * RADIUS_BOX
ROWS = 2 * F
REC = 24
BLOCK = 32
ROUNDER = 12582912.0

COS = (
    0.9999992216144897,
    -19.738982519159087,
    64.9287266658944,
    -85.27239730229532,
    58.794039342441934,
    -21.076782244925596,
)
SIN = (
    6.283055797987737,
    -41.33121426662637,
    81.36681462152343,
    -74.47800045497374,
    32.7813926131928,
)
MESH = pl.DeviceIdType.MESH


def horner(coefficients, z):
    total = coefficients[-1]
    for coefficient in coefficients[-2::-1]:
        total = total * z + coefficient
    return total


def geometry(target, cols):
    squared = SOFT * SOFT
    for axis in range(3):
        offset = target[axis] - cols[:, ROWS + axis : ROWS + axis + 1]
        squared = squared + offset * offset
    inverse = lax.rsqrt(squared)
    distance = squared * inverse
    distance = distance + (0.5 * inverse) * (squared - distance * distance)
    return distance, inverse


def point_terms(distance, inverse, turns, real, imag):
    phase = distance * turns
    phase = phase - ((phase + ROUNDER) - ROUNDER)
    z = phase * phase
    cosine = inverse * horner(COS, z)
    sine = (inverse * phase) * horner(SIN, z)
    return cosine * real - sine * imag, cosine * imag + sine * real


def fold(block):
    return block.reshape(block.shape[0] // 8, 8, block.shape[1]).sum(0)


def zeros_acc(count):
    return tuple(jnp.zeros((8, 128), jnp.float32) for _ in range(2 * count))


def apply_points(target, load, turns, acc):
    def step(block, acc):
        cols = load(block)
        distance, inverse = geometry(target, cols)
        out = list(acc)
        for f in range(F):
            re, im = point_terms(
                distance, inverse, turns[f], cols[:, f : f + 1], cols[:, F + f : F + f + 1]
            )
            out[f] = out[f] + fold(re)
            out[F + f] = out[F + f] + fold(im)
        return tuple(out)

    return lax.fori_loop(0, LEAF // BLOCK, step, acc, unroll=True)


def rows_of(acc):
    return jnp.concatenate([jnp.sum(a, axis=0, keepdims=True) for a in acc], axis=0)


def kernel(
    sec_size,
    dev_size,
    groups,
    wave_ref,
    centers_ref,
    group_centers_ref,
    pairs_ref,
    counts_ref,
    lists_ref,
    group_lists_ref,
    sources_ref,
    positions_ref,
    weights_ref,
    directions_ref,
    result_ref,
    rayleigh_ref,
    window,
    records,
    targets_xyz,
    dir_cols,
    scratch_rec,
    multipole,
    gathered,
    contribution,
    contributions,
    group_send,
    group_multipoles,
    local_send,
    group_locals,
    near,
    box_local,
    sums_send,
    sums,
    halo_send_sem,
    halo_recv_sem,
    gather_send_sem,
    gather_recv_sem,
    up_send_sem,
    up_recv_sem,
    across_send_sem,
    across_recv_sem,
    down_send_sem,
    down_recv_sem,
    sums_send_sem,
    sums_recv_sem,
):
    count = sec_size * dev_size
    me = lax.axis_index("sec") * dev_size + lax.axis_index("dev")
    group = me // GROUP
    member = me % GROUP

    def place(device):
        return (device // dev_size, device % dev_size)

    barrier = pltpu.get_barrier_semaphore()

    def greet(step, carry):
        pl.semaphore_signal(
            barrier, inc=1, device_id=place((me + step) % count), device_id_type=MESH
        )
        return carry

    lax.fori_loop(1, count, greet, 0)

    turns = [wave_ref[f] * (0.5 / math.pi) for f in range(F)]

    weighted = sources_ref[...] * weights_ref[...]
    own_rows = jnp.concatenate(
        [weighted, positions_ref[...], jnp.zeros((REC - ROWS - 3, P_DEV), jnp.float32)], axis=0
    )
    window[1] = own_rows
    for leaf in range(LEAVES):
        part = own_rows[:, leaf * LEAF : (leaf + 1) * LEAF]
        records[LEAVES + leaf] = part.T
        targets_xyz[leaf] = part[ROWS : ROWS + 8]
    directions = directions_ref[...]
    dir_rows = jnp.concatenate([directions, jnp.zeros((5, Q), jnp.float32)], axis=0)
    dir_cols[...] = dir_rows.T

    def proxies(centers, index, radius):
        return [centers[axis, index] + radius * directions[axis : axis + 1] for axis in range(3)]

    own_proxies = proxies(centers_ref, me, RADIUS_BOX)
    parent_proxies = proxies(group_centers_ref, group, RADIUS_GROUP)
    row_padding = jnp.zeros((REC - ROWS - 3, Q), jnp.float32)

    def set_records(slot, rows, xyz):
        scratch_rec[slot] = jnp.concatenate([rows, *xyz, row_padding], axis=0).T

    def loader(ref, index):
        return lambda block: ref[index, pl.ds(pl.multiple_of(block * BLOCK, BLOCK), BLOCK), :]

    def outward_leaf(leaf, acc):
        return apply_points(own_proxies, loader(records, LEAVES + leaf), turns, acc)

    outward = lax.fori_loop(0, LEAVES, outward_leaf, zeros_acc(F))
    own_multipole = rows_of(outward) * (RADIUS_BOX / math.sqrt(P_DEV))
    multipole[...] = own_multipole
    gathered[me] = own_multipole

    pl.semaphore_wait(barrier, count - 1)

    after = (me + 1) % count
    before = (me + count - 1) % count
    halos = [
        pltpu.make_async_remote_copy(
            src_ref=window.at[1],
            dst_ref=window.at[slot],
            send_sem=halo_send_sem.at[way],
            recv_sem=halo_recv_sem.at[way],
            device_id=place(device),
            device_id_type=MESH,
        )
        for way, (slot, device) in enumerate(((0, after), (2, before)))
    ]
    for halo in halos:
        halo.start()

    def send_to(src, dst, send_sem, recv_sem, device):
        pltpu.make_async_remote_copy(
            src_ref=src,
            dst_ref=dst,
            send_sem=send_sem,
            recv_sem=recv_sem,
            device_id=place(device),
            device_id_type=MESH,
        ).start()

    def wait_bytes(ref, pieces, sem):
        part = ref.at[pl.ds(0, pieces)]
        pltpu.make_async_copy(part, part, sem).wait()

    def send_multipole(step, carry):
        send_to(
            multipole, gathered.at[me], gather_send_sem, gather_recv_sem, (me + step) % count
        )
        return carry

    set_records(0, own_multipole, own_proxies)
    terms = rows_of(
        apply_points(parent_proxies, loader(scratch_rec, 0), turns, zeros_acc(F))
    ) * (RADIUS_GROUP / math.sqrt(GROUP * Q))
    padding = jnp.zeros((6, Q), jnp.float32)
    for f in range(F):
        contribution[f] = jnp.concatenate(
            [terms[f : f + 1], terms[F + f : F + f + 1], padding], axis=0
        )
    contributions[member] = contribution[member]

    def send_up(step, carry):
        other = (member + step) % GROUP
        send_to(
            contribution.at[other],
            contributions.at[member],
            up_send_sem,
            up_recv_sem,
            group * GROUP + other,
        )
        return carry

    lax.fori_loop(1, GROUP, send_up, 0)
    lax.fori_loop(1, count, send_multipole, 0)

    for way, halo in enumerate(halos):
        halo.wait_recv()
        slot = 2 * way
        inside = jnp.where(me > 0, 1.0, 0.0) if way == 0 else jnp.where(me < count - 1, 1.0, 0.0)
        rows = window[slot]
        rows = jnp.concatenate([rows[:ROWS] * inside, rows[ROWS:]], axis=0)
        for leaf in range(LEAVES):
            records[slot * LEAVES + leaf] = rows[:, leaf * LEAF : (leaf + 1) * LEAF].T
    near[...] = jnp.zeros_like(near)

    def near_pair(pair, carry):
        target = pairs_ref[0, pair]
        anchor = pairs_ref[1, pair]
        live = jnp.where(pair < counts_ref[0], 1.0, 0.0)
        xyz = targets_xyz[target]
        rows = rows_of(
            apply_points(
                [xyz[axis : axis + 1] for axis in range(3)],
                loader(records, anchor),
                turns,
                zeros_acc(F),
            )
        )
        for leaf in range(LEAVES):
            near[leaf] += rows * jnp.where(target == leaf, live, 0.0)
        return carry

    first_half = PAIRS_MAX // 2
    lax.fori_loop(0, first_half, near_pair, 0)

    wait_bytes(contributions, GROUP - 1, up_recv_sem)
    total = contributions[0]
    for other in range(1, GROUP):
        total = total + contributions[other]
    group_send[...] = total
    group_multipoles[group] = total

    def send_across(step, carry):
        send_to(
            group_send,
            group_multipoles.at[group],
            across_send_sem,
            across_recv_sem,
            (me + step * GROUP) % count,
        )
        return carry

    if groups > 1:
        lax.fori_loop(1, groups, send_across, 0)

    lax.fori_loop(first_half, PAIRS_MAX, near_pair, 0)

    if groups > 1:
        wait_bytes(group_multipoles, groups - 1, across_recv_sem)
    my_turns = wave_ref[member] * (0.5 / math.pi)
    local_acc = zeros_acc(1)
    for m in range(ML2):
        other = group_lists_ref[group, m]
        rows = group_multipoles[other]
        xyz = proxies(group_centers_ref, other, RADIUS_GROUP)
        cols = jnp.concatenate([rows, rows, *xyz, row_padding], axis=0).T
        for block in range(Q // BLOCK):
            part = cols[block * BLOCK : (block + 1) * BLOCK]
            distance, inverse = geometry(parent_proxies, part)
            re, im = point_terms(distance, inverse, my_turns, part[:, 0:1], part[:, 1:2])
            local_acc = (local_acc[0] + fold(re), local_acc[1] + fold(im))
    local = jnp.concatenate([rows_of(local_acc), padding], axis=0) * (
        RADIUS_GROUP / math.sqrt(ML2 * Q)
    )
    local_send[...] = local
    group_locals[member] = local

    def send_down(step, carry):
        send_to(
            local_send,
            group_locals.at[member],
            down_send_sem,
            down_recv_sem,
            group * GROUP + (member + step) % GROUP,
        )
        return carry

    lax.fori_loop(1, GROUP, send_down, 0)

    wait_bytes(gathered, count - 1, gather_recv_sem)

    def list_box(m, acc):
        other = lists_ref[0, m]
        set_records(0, gathered[other], proxies(centers_ref, other, RADIUS_BOX))
        return apply_points(own_proxies, loader(scratch_rec, 0), turns, acc)

    incoming = lax.fori_loop(0, ML1, list_box, zeros_acc(F))
    incoming = rows_of(incoming) * (RADIUS_BOX / math.sqrt(ML1 * Q))

    wait_bytes(group_locals, GROUP - 1, down_recv_sem)
    rows = jnp.concatenate(
        [group_locals[f][part : part + 1] for part in range(2) for f in range(F)], axis=0
    )
    set_records(0, rows, parent_proxies)
    descended = rows_of(
        apply_points(own_proxies, loader(scratch_rec, 0), turns, zeros_acc(F))
    ) * (RADIUS_GROUP / math.sqrt(Q))
    set_records(0, incoming + descended, own_proxies)

    def far_leaf(leaf, carry):
        xyz = targets_xyz[leaf]
        rows = rows_of(
            apply_points(
                [xyz[axis : axis + 1] for axis in range(3)],
                loader(scratch_rec, 0),
                turns,
                zeros_acc(F),
            )
        )
        near[leaf] = near[leaf] * (1.0 / math.sqrt(LEAF * PAIRS_LEAF)) + rows * (
            RADIUS_BOX / math.sqrt(Q)
        )
        return carry

    lax.fori_loop(0, LEAVES, far_leaf, 0)
    sources = sources_ref[...]
    result = 0.5 * sources + jnp.concatenate([near[leaf] for leaf in range(LEAVES)], axis=1)
    result_ref[...] = result

    s_re, s_im = sources[:F], sources[F:]
    r_re, r_im = result[:F], result[F:]
    real_sum = jnp.sum(s_re * r_re + s_im * r_im, axis=1, keepdims=True)
    imag_sum = jnp.sum(s_re * r_im - s_im * r_re, axis=1, keepdims=True)
    squares = jnp.sum(s_re * s_re + s_im * s_im, axis=1, keepdims=True)
    lane = lax.broadcasted_iota(jnp.int32, (F, 128), 1)
    mine = jnp.where(
        lane == 0, real_sum, jnp.where(lane == 1, imag_sum, jnp.where(lane == 2, squares, 0.0))
    )
    sums_send[...] = mine
    sums[me] = mine

    def send_sums(step, carry):
        send_to(sums_send, sums.at[me], sums_send_sem, sums_recv_sem, (me + step) % count)
        return carry

    lax.fori_loop(1, count, send_sums, 0)

    for halo in halos:
        halo.wait_send()
    wait_bytes(gathered, count - 1, gather_send_sem)
    wait_bytes(contributions, GROUP - 1, up_send_sem)
    if groups > 1:
        wait_bytes(group_multipoles, groups - 1, across_send_sem)
    wait_bytes(group_locals, GROUP - 1, down_send_sem)
    wait_bytes(sums, count - 1, sums_recv_sem)
    total = jnp.sum(sums[...], axis=0).T
    rayleigh_ref[...] = total[0:2, :] / (total[2:3, :] + 1e-06)
    wait_bytes(sums, count - 1, sums_send_sem)


def on_device(
    sec_size,
    dev_size,
    sources,
    positions,
    weights,
    wavenumbers,
    directions,
    box_centers,
    group_centers,
    near_pairs,
    pair_counts,
    box_lists,
    group_lists,
):
    count = sec_size * dev_size
    groups = count // GROUP
    smem = pl.BlockSpec(memory_space=pltpu.SMEM)
    vmem = pl.BlockSpec(memory_space=pltpu.VMEM)
    f32 = jnp.float32
    result, rayleigh = pl.pallas_call(
        functools.partial(kernel, sec_size, dev_size, groups),
        out_shape=(
            jax.ShapeDtypeStruct((ROWS, P_DEV), f32),
            jax.ShapeDtypeStruct((2, F), f32),
        ),
        in_specs=[smem] * 7 + [vmem] * 4,
        out_specs=(vmem, vmem),
        scratch_shapes=[
            pltpu.VMEM((3, REC, P_DEV), f32),
            pltpu.VMEM((3 * LEAVES, LEAF, REC), f32),
            pltpu.VMEM((LEAVES, 8, LEAF), f32),
            pltpu.VMEM((Q, 8), f32),
            pltpu.VMEM((1, Q, REC), f32),
            pltpu.VMEM((ROWS, Q), f32),
            pltpu.VMEM((count, ROWS, Q), f32),
            pltpu.VMEM((F, 8, Q), f32),
            pltpu.VMEM((GROUP, 8, Q), f32),
            pltpu.VMEM((8, Q), f32),
            pltpu.VMEM((groups, 8, Q), f32),
            pltpu.VMEM((8, Q), f32),
            pltpu.VMEM((GROUP, 8, Q), f32),
            pltpu.VMEM((LEAVES, ROWS, LEAF), f32),
            pltpu.VMEM((ROWS, Q), f32),
            pltpu.VMEM((F, 128), f32),
            pltpu.VMEM((count, F, 128), f32),
            pltpu.SemaphoreType.DMA((2,)),
            pltpu.SemaphoreType.DMA((2,)),
        ]
        + [pltpu.SemaphoreType.DMA] * 10,
        compiler_params=pltpu.CompilerParams(
            collective_id=0, has_side_effects=True, vmem_limit_bytes=32 * 1024 * 1024
        ),
        name="bem_matvec",
    )(
        wavenumbers,
        box_centers,
        group_centers,
        near_pairs[0],
        pair_counts,
        box_lists,
        group_lists,
        sources.reshape(ROWS, P_DEV),
        positions,
        weights[None, :],
        directions,
    )
    return result.reshape(2, F, P_DEV), rayleigh


def solution(mesh):
    in_specs = (
        P(None, None, ("sec", "dev")),
        P(None, ("sec", "dev")),
        P(("sec", "dev")),
        P(),
        P(),
        P(),
        P(),
        P(("sec", "dev"), None, None),
        P(("sec", "dev")),
        P(("sec", "dev"), None),
        P(),
    )
    out_specs = (P(None, None, ("sec", "dev")), P())
    return jax.shard_map(
        functools.partial(on_device, mesh.shape["sec"], mesh.shape["dev"]),
        mesh=mesh,
        in_specs=in_specs,
        out_specs=out_specs,
        check_vma=False,
    )
```

time: 390 us -> 36.6 us (0.09)
  blocking collectives: 189 us -> 0 us
  matrix products: 170 us -> 0 us
  Pallas kernels: 0 us -> 30.2 us
  other arithmetic: 7.43 us -> 0 us
  loops' own time: 6.52 us -> 0 us
  starting transfers between devices: 4.31 us -> 0 us
    dot_general x34 -> x0, matrix products: 170 us -> none  [the longest x7 46.7 us: apply_block(): jnp.einsum('fab,fb->fa', real_kernel, values[1], precision=highest)]
    psum x1 -> x0, blocking collectives: 107 us -> none  [on_device(): lax.psum((jnp.stack([real_sum, imag_sum]), squares), ('sec', 'dev'))]
    all_gather x2 -> x0, blocking collectives: 81.3 us -> none  [the longest x1 43.9 us: on_device(): lax.all_gather(contribution[None], ('sec', 'dev'), axis=0, tiled=True)]
    pallas_call x0 -> x1, Pallas kernels: none -> 30.2 us  [on_device(): pl.pallas_call(functools.partial(kernel, sec_size, dev_size, groups), out...]
    another operation x1 -> x0, loops' own time: 6.52 us -> none  [on_device(): lax.fori_loop(0, turn_count, near_turn, jnp.zeros((2, F, LEAVES, LEAF), j...]
    gather x10 -> x0, local copies, waits for them, and re-layouts: 5.59 us -> none  [the longest x2 1.14 us: near_turn(): window_xyz[:, anchor_ids]]
    unnamed x20 -> x21, local copies, waits for them, and re-layouts: 0.24 us -> 4.7 us
    ppermute x2 -> x0, starting transfers between devices: 4.31 us -> none  [the longest x1 3.03 us: with_halo(): lax.ppermute(tail, axis, [(i, (i + 1) % count) for i in range(ends)])]
  transfers between devices with their start and end apart: 2 -> 0, of which waited for: 0 -> 0; matrix products, arithmetic and copies ran while one was open for 35% -> 0% of each run, Pallas kernels for 0% -> 0%
where the time goes in v1:
time: 36.6 us; the launch traced here: 36.3 us
  Pallas kernels  30.2 us (83%)
  local copies, waits for them, and re-layouts  4.7 us (13%)
  between operations  1.37 us (4%)
    pallas_call x1, Pallas kernels, on_device(): pl.pallas_call(functools.partial(kernel, sec_size, dev_size, groups), out...  30.2 us
    unnamed x21, local copies, waits for them, and re-layouts  4.7 us

profile of v1, /device:TPU:0, one launch (start us, length us, event | category | flops | bytes accessed | tf_op | source)
XLA Modules:
  0.0 36.3 jit_solution(12809225161663988013)
XLA Ops:
  0.6 0.0 copy-start.4
  1.3 0.0 copy-start.1
  1.3 0.0 copy-start.2
  1.3 0.0 copy-start.3
  1.3 0.0 copy-start.7
  1.3 0.8 %copy.13.group_lists_ref = s32[4,2]{1,0:T(4,128)S(1)} copy(s32[4,2]{0,1:T(2,128)} %param.21) | data formatting | bytes 64 | tf_op args[10]
  2.1 0.0 copy-done.4
  2.1 0.0 copy-done.1
  2.1 0.0 copy-done.2
  2.1 0.0 copy-done.3
  2.1 0.0 copy-done.7
  2.2 0.0 copy-start
  2.2 0.7 %copy-done = f32[2,8,256]{2,1,0:T(8,128)S(1)} copy-done((f32[2,8,256]{2,1,0:T(8,128)S(1)}, f32[2,8,256]{2,1,0:T(8,128)}, u32[]{:S(2)}) %copy-start) | copy-done | bytes 16408
  2.9 0.0 copy-start.5
  2.9 0.7 %copy-done.5 = s32[1,2,10]{2,1,0:T(2,128)S(1)} copy-done((s32[1,2,10]{2,1,0:T(2,128)S(1)}, s32[1,2,10]{2,1,0:T(2,128)}, u32[]{:S(2)}) %copy-start.5) | copy-done | bytes 104
  3.6 0.0 copy-start.6
  3.6 0.7 %copy-done.6 = f32[256]{0:T(256)S(1)} copy-done((f32[256]{0:T(256)S(1)}, f32[256]{0:T(256)}, u32[]{:S(2)}) %copy-start.6) | copy-done | bytes 1048
  4.2 0.0 copy-start.8
  4.2 0.7 %copy-done.8 = s32[1,4]{1,0:T(1,128)S(1)} copy-done((s32[1,4]{1,0:T(1,128)S(1)}, s32[1,4]{1,0:T(1,128)}, u32[]{:S(2)}) %copy-start.8) | copy-done | bytes 40
  4.9 30.2 %bem_matvec.1 = (f32[16,256]{1,0:T(8,128)S(1)}, f32[2,8]{1,0:T(2,128)S(1)}) custom-call(f32[8]{0:T(128)S(1)} %copy-done.7, f32[3,32]{1,0:T(4,128)S(1)} %copy-done.2, f32[3,4]{1,0:T(4,128)S(1)} %copy-done.3, s32[2,10]{1,0:T(2,128)S(1)} %bitcast.6, s32[1]{0:T(128)S(6)} %copy.16.counts_ref, s32[1,4]{1,0:T(1,128)S(1)} %copy-done.8, ...), custom_call_target="tpu_custom_call" | custom-call | tf_op jit(solution)/shard_map/bem_matvec/pallas_call | solution.py:442
  35.1 0.6 %copy.17 = f32[2,8,256]{2,1,0:T(8,128)} copy(f32[2,8,256]{2,1,0:T(8,128)S(1)} %bitcast.5) | data formatting | bytes 32768
  35.7 0.6 %copy.18 = f32[2,8]{1,0:T(2,128)} copy(f32[2,8]{1,0:T(2,128)S(1)} %get-tuple-element.9) | data formatting | bytes 128
Async XLA Ops:
  0.6 1.5 %copy-start.4 = (f32[3,128]{1,0:T(4,128)S(1)}, f32[3,128]{1,0:T(4,128)}, u32[]{:S(2)}) copy-start(f32[3,128]{1,0:T(4,128)} %directions_ref.1) | copy-start | bytes 4612
  1.3 0.8 %copy-start.1 = (f32[3,256]{1,0:T(4,128)S(1)}, f32[3,256]{1,0:T(4,128)}, u32[]{:S(2)}) copy-start(f32[3,256]{1,0:T(4,128)} %positions_ref.1) | copy-start | bytes 9220
  1.3 0.8 %copy-start.2 = (f32[3,32]{1,0:T(4,128)S(1)}, f32[3,32]{1,0:T(4,128)}, u32[]{:S(2)}) copy-start(f32[3,32]{1,0:T(4,128)} %centers_ref.1) | copy-start | bytes 1156
  1.3 0.8 %copy-start.3 = (f32[3,4]{1,0:T(4,128)S(1)}, f32[3,4]{1,0:T(4,128)}, u32[]{:S(2)}) copy-start(f32[3,4]{1,0:T(4,128)} %group_centers_ref.1) | copy-start | bytes 148
  1.3 0.8 %copy-start.7 = (f32[8]{0:T(128)S(1)}, f32[8]{0:T(128)}, u32[]{:S(2)}) copy-start(f32[8]{0:T(128)} %wave_ref.1) | copy-start | bytes 100
  2.2 0.7 %copy-start = (f32[2,8,256]{2,1,0:T(8,128)S(1)}, f32[2,8,256]{2,1,0:T(8,128)}, u32[]{:S(2)}) copy-start(f32[2,8,256]{2,1,0:T(8,128)} %param.11) | copy-start | bytes 49156
  2.9 0.7 %copy-start.5 = (s32[1,2,10]{2,1,0:T(2,128)S(1)}, s32[1,2,10]{2,1,0:T(2,128)}, u32[]{:S(2)}) copy-start(s32[1,2,10]{2,1,0:T(2,128)} %param.18) | copy-start | bytes 244
  3.6 0.7 %copy-start.6 = (f32[256]{0:T(256)S(1)}, f32[256]{0:T(256)}, u32[]{:S(2)}) copy-start(f32[256]{0:T(256)} %param.13) | copy-start | bytes 3076
  4.2 0.7 %copy-start.8 = (s32[1,4]{1,0:T(1,128)S(1)}, s32[1,4]{1,0:T(1,128)}, u32[]{:S(2)}) copy-start(s32[1,4]{1,0:T(1,128)} %lists_ref.1) | copy-start | bytes 52

commit v2 on v1

v2 whole, which is shorter than its diff:
```python
import functools
import math

import jax
import jax.numpy as jnp
from jax import lax
from jax.experimental import pallas as pl
from jax.experimental.pallas import tpu as pltpu
from jax.sharding import PartitionSpec as P

LEAF = 128
LEAVES = 2
F = 8
Q = 128
PAIRS_LEAF = 5
ML1 = 4
ML2 = 2
GROUP = 8
P_DEV = 256
PAIRS_MAX = 10

SOFT = 0.1
RADIUS_BOX = 1.0 + 0.5 * LEAVES
RADIUS_GROUP = 2.0 * RADIUS_BOX
ROWS = 2 * F
REC = 24
BLOCK = 32
ROUNDER = 12582912.0

COS = (
    0.9999992216144897,
    -19.738982519159087,
    64.9287266658944,
    -85.27239730229532,
    58.794039342441934,
    -21.076782244925596,
)
SIN = (
    6.283055797987737,
    -41.33121426662637,
    81.36681462152343,
    -74.47800045497374,
    32.7813926131928,
)
MESH = pl.DeviceIdType.MESH


def horner(coefficients, z):
    total = coefficients[-1]
    for coefficient in coefficients[-2::-1]:
        total = total * z + coefficient
    return total


def geometry(target, cols):
    squared = SOFT * SOFT
    for axis in range(3):
        offset = target[axis] - cols[:, ROWS + axis : ROWS + axis + 1]
        squared = squared + offset * offset
    inverse = lax.rsqrt(squared)
    distance = squared * inverse
    distance = distance + (0.5 * inverse) * (squared - distance * distance)
    return distance, inverse


def point_terms(distance, inverse, turns, real, imag):
    phase = distance * turns
    phase = phase - ((phase + ROUNDER) - ROUNDER)
    z = phase * phase
    cosine = inverse * horner(COS, z)
    sine = (inverse * phase) * horner(SIN, z)
    return cosine * real - sine * imag, cosine * imag + sine * real


def fold(block):
    return block.reshape(block.shape[0] // 8, 8, block.shape[1]).sum(0)


def apply_points(geo, target, load, turns, add):
    blocks = range(LEAF // BLOCK)
    for block in blocks:
        distance, inverse = geometry(target, load(block))
        geo[0, pl.ds(block * BLOCK, BLOCK), :] = distance
        geo[1, pl.ds(block * BLOCK, BLOCK), :] = inverse
    for f in range(F):
        total_re, total_im = 0.0, 0.0
        for block in blocks:
            cols = load(block)
            re, im = point_terms(
                geo[0, pl.ds(block * BLOCK, BLOCK), :],
                geo[1, pl.ds(block * BLOCK, BLOCK), :],
                turns[f],
                cols[:, f : f + 1],
                cols[:, F + f : F + f + 1],
            )
            total_re = total_re + fold(re)
            total_im = total_im + fold(im)
        add(f, total_re)
        add(F + f, total_im)


def adder(ref, first=False):
    def add(row, term):
        ref[row] = term if first else ref[row] + term

    return add


def rows_of(acc):
    return jnp.sum(acc, axis=1)


def wrapped(index, size):
    return jnp.where(index >= size, index - size, index)


def kernel(
    sec_size,
    dev_size,
    groups,
    wave_hbm,
    centers_hbm,
    group_centers_hbm,
    pairs_hbm,
    counts_hbm,
    lists_hbm,
    group_lists_hbm,
    sources_hbm,
    positions_hbm,
    weights_hbm,
    directions_hbm,
    result_ref,
    rayleigh_ref,
    wave_ref,
    centers_ref,
    group_centers_ref,
    pairs_ref,
    counts_ref,
    lists_ref,
    group_lists_ref,
    sources_ref,
    positions_ref,
    weights_ref,
    directions_ref,
    geo,
    acc,
    window,
    records,
    targets_xyz,
    scratch_rec,
    gathered,
    contribution,
    contributions,
    group_send,
    group_multipoles,
    local_send,
    group_locals,
    near,
    sums_send,
    sums,
    totals_send,
    totals,
    operand_sem,
    halo_send_sem,
    halo_recv_sem,
    wide_send_sem,
    wide_recv_sem,
    gather_send_sem,
    gather_recv_sem,
    up_send_sem,
    up_recv_sem,
    across_send_sem,
    across_recv_sem,
    down_send_sem,
    down_recv_sem,
    sums_send_sem,
    sums_recv_sem,
    totals_send_sem,
    totals_recv_sem,
):
    count = sec_size * dev_size
    sec, dev = lax.axis_index("sec"), lax.axis_index("dev")
    me = sec * dev_size + dev
    per_row = dev_size // GROUP
    group = me // GROUP
    member = dev % GROUP
    first = dev - member
    mates = [wrapped(member + step, GROUP) for step in range(1, GROUP)]
    mate_places = [(sec, first + mate) for mate in mates]
    far_places = [
        (wrapped(sec + row, sec_size), wrapped(dev + column * GROUP, dev_size))
        for row in range(sec_size)
        for column in range(per_row)
        if row or column
    ]
    last, begin = dev == dev_size - 1, dev == 0
    after = (
        jnp.where(last, wrapped(sec + 1, sec_size), sec),
        jnp.where(last, 0, dev + 1),
    )
    before = (
        jnp.where(begin, wrapped(sec + sec_size - 1, sec_size), sec),
        jnp.where(begin, dev_size - 1, dev - 1),
    )

    operands = [
        pltpu.make_async_copy(src, dst, operand_sem.at[index])
        for index, (src, dst) in enumerate(
            (
                (sources_hbm, sources_ref),
                (weights_hbm, weights_ref),
                (positions_hbm, positions_ref),
                (directions_hbm, directions_ref),
                (wave_hbm, wave_ref),
                (centers_hbm, centers_ref),
                (group_centers_hbm, group_centers_ref),
                (pairs_hbm, pairs_ref),
                (counts_hbm, counts_ref),
                (lists_hbm, lists_ref),
                (group_lists_hbm, group_lists_ref),
            )
        )
    ]
    for operand in operands:
        operand.start()

    barrier = pltpu.get_barrier_semaphore()
    partners = mate_places + far_places + [after, before]
    for partner in partners:
        pl.semaphore_signal(barrier, inc=1, device_id=partner, device_id_type=MESH)
    for operand in operands:
        operand.wait()

    turns = [wave_ref[f] * (0.5 / math.pi) for f in range(F)]

    weighted = sources_ref[...] * weights_ref[...]
    own_rows = jnp.concatenate(
        [weighted, positions_ref[...], jnp.zeros((REC - ROWS - 3, P_DEV), jnp.float32)], axis=0
    )
    window[1] = own_rows
    for leaf in range(LEAVES):
        part = own_rows[:, leaf * LEAF : (leaf + 1) * LEAF]
        records[LEAVES + leaf] = part.T
        targets_xyz[leaf] = part[ROWS : ROWS + 8]
    directions = directions_ref[...]

    def proxies(centers, index, radius):
        return [centers[axis, index] + radius * directions[axis : axis + 1] for axis in range(3)]

    own_proxies = proxies(centers_ref, me, RADIUS_BOX)
    parent_proxies = proxies(group_centers_ref, group, RADIUS_GROUP)
    row_padding = jnp.zeros((REC - ROWS - 3, Q), jnp.float32)

    def set_records(slot, rows, xyz):
        scratch_rec[slot] = jnp.concatenate([rows, *xyz, row_padding], axis=0).T

    def loader(ref, index):
        return lambda block: ref[index, pl.ds(pl.multiple_of(block * BLOCK, BLOCK), BLOCK), :]

    acc[...] = jnp.zeros_like(acc)

    def outward_leaf(leaf, carry):
        apply_points(geo, own_proxies, loader(records, LEAVES + leaf), turns, adder(acc))
        return carry

    lax.fori_loop(0, LEAVES, outward_leaf, 0)
    own_multipole = rows_of(acc[...]) * (RADIUS_BOX / math.sqrt(P_DEV))
    gathered[member, group] = own_multipole

    pl.semaphore_wait(barrier, len(partners))

    halos = [
        pltpu.make_async_remote_copy(
            src_ref=window.at[1],
            dst_ref=window.at[slot],
            send_sem=halo_send_sem.at[way],
            recv_sem=halo_recv_sem.at[way],
            device_id=device,
            device_id_type=MESH,
        )
        for way, (slot, device) in enumerate(((0, after), (2, before)))
    ]
    for halo in halos:
        halo.start()

    def send_to(src, dst, send_sem, recv_sem, device):
        pltpu.make_async_remote_copy(
            src_ref=src,
            dst_ref=dst,
            send_sem=send_sem,
            recv_sem=recv_sem,
            device_id=device,
            device_id_type=MESH,
        ).start()

    def wait_bytes(ref, pieces, sem):
        part = ref.at[pl.ds(0, pieces)]
        pltpu.make_async_copy(part, part, sem).wait()

    own_slot = gathered.at[member, group]
    for device in far_places:
        send_to(own_slot, own_slot, wide_send_sem, wide_recv_sem, device)

    set_records(0, own_multipole, own_proxies)
    apply_points(geo, parent_proxies, loader(scratch_rec, 0), turns, adder(acc, True))
    terms = rows_of(acc[...]) * (RADIUS_GROUP / math.sqrt(GROUP * Q))
    padding = jnp.zeros((6, Q), jnp.float32)
    for f in range(F):
        contribution[f] = jnp.concatenate(
            [terms[f : f + 1], terms[F + f : F + f + 1], padding], axis=0
        )
    contributions[member] = contribution[member]
    for mate, device in zip(mates, mate_places):
        send_to(
            contribution.at[mate], contributions.at[member], up_send_sem, up_recv_sem, device
        )

    for way, halo in enumerate(halos):
        halo.wait_recv()
        slot = 2 * way
        inside = jnp.where(me > 0, 1.0, 0.0) if way == 0 else jnp.where(me < count - 1, 1.0, 0.0)
        rows = window[slot]
        rows = jnp.concatenate([rows[:ROWS] * inside, rows[ROWS:]], axis=0)
        for leaf in range(LEAVES):
            records[slot * LEAVES + leaf] = rows[:, leaf * LEAF : (leaf + 1) * LEAF].T
    near[...] = jnp.zeros_like(near)

    def near_pair(pair, carry):
        target = pairs_ref[0, 0, pair]
        anchor = pairs_ref[0, 1, pair]
        live = jnp.where(pair < counts_ref[0], 1.0, 0.0)
        xyz = targets_xyz[target]
        lives = [jnp.where(target == leaf, live, 0.0) for leaf in range(LEAVES)]

        def add(row, term):
            for leaf in range(LEAVES):
                near[leaf, row] += term * lives[leaf]

        apply_points(
            geo, [xyz[axis : axis + 1] for axis in range(3)], loader(records, anchor), turns, add
        )
        return carry

    first_half = PAIRS_MAX // 2
    lax.fori_loop(0, first_half, near_pair, 0)

    wait_bytes(contributions, GROUP - 1, up_recv_sem)
    total = contributions[0]
    for other in range(1, GROUP):
        total = total + contributions[other]
    group_send[...] = total
    group_multipoles[group] = total

    for device in far_places:
        send_to(
            group_send, group_multipoles.at[group], across_send_sem, across_recv_sem, device
        )

    if groups > 1:
        wait_bytes(gathered.at[0], groups - 1, wide_recv_sem)
    own_part = gathered.at[member]
    for device in mate_places:
        send_to(own_part, own_part, gather_send_sem, gather_recv_sem, device)

    lax.fori_loop(first_half, PAIRS_MAX, near_pair, 0)

    if groups > 1:
        wait_bytes(group_multipoles, groups - 1, across_recv_sem)
    my_turns = wave_ref[member] * (0.5 / math.pi)
    local_re, local_im = 0.0, 0.0
    for m in range(ML2):
        other = group_lists_ref[m, group]
        rows = group_multipoles[other]
        xyz = proxies(group_centers_ref, other, RADIUS_GROUP)
        cols = jnp.concatenate([rows, rows, *xyz, row_padding], axis=0).T
        for block in range(Q // BLOCK):
            part = cols[block * BLOCK : (block + 1) * BLOCK]
            distance, inverse = geometry(parent_proxies, part)
            re, im = point_terms(distance, inverse, my_turns, part[:, 0:1], part[:, 1:2])
            local_re = local_re + fold(re)
            local_im = local_im + fold(im)
    local_rows = [jnp.sum(part, axis=0, keepdims=True) for part in (local_re, local_im)]
    local = jnp.concatenate([*local_rows, padding], axis=0) * (
        RADIUS_GROUP / math.sqrt(ML2 * Q)
    )
    local_send[...] = local
    group_locals[member] = local

    for device in mate_places:
        send_to(local_send, group_locals.at[member], down_send_sem, down_recv_sem, device)

    wait_bytes(gathered, GROUP - 1, gather_recv_sem)
    acc[...] = jnp.zeros_like(acc)

    def list_box(m, carry):
        other = lists_ref[0, m]
        set_records(
            0, gathered[other % GROUP, other // GROUP], proxies(centers_ref, other, RADIUS_BOX)
        )
        apply_points(geo, own_proxies, loader(scratch_rec, 0), turns, adder(acc))
        return carry

    lax.fori_loop(0, ML1, list_box, 0)
    incoming = rows_of(acc[...]) * (RADIUS_BOX / math.sqrt(ML1 * Q))

    wait_bytes(group_locals, GROUP - 1, down_recv_sem)
    rows = jnp.concatenate(
        [group_locals[f][part : part + 1] for part in range(2) for f in range(F)], axis=0
    )
    set_records(0, rows, parent_proxies)
    apply_points(geo, own_proxies, loader(scratch_rec, 0), turns, adder(acc, True))
    descended = rows_of(acc[...]) * (RADIUS_GROUP / math.sqrt(Q))
    set_records(0, incoming + descended, own_proxies)

    def far_leaf(leaf, carry):
        xyz = targets_xyz[leaf]

        def add(row, term):
            near[leaf, row] = near[leaf, row] * (1.0 / math.sqrt(LEAF * PAIRS_LEAF)) + term * (
                RADIUS_BOX / math.sqrt(Q)
            )

        apply_points(
            geo, [xyz[axis : axis + 1] for axis in range(3)], loader(scratch_rec, 0), turns, add
        )
        return carry

    lax.fori_loop(0, LEAVES, far_leaf, 0)
    sources = sources_ref[...]
    result = 0.5 * sources + jnp.concatenate([rows_of(near[leaf]) for leaf in range(LEAVES)], axis=1)
    result_ref[...] = result

    s_re, s_im = sources[:F], sources[F:]
    r_re, r_im = result[:F], result[F:]
    real_sum = jnp.sum(s_re * r_re + s_im * r_im, axis=1, keepdims=True)
    imag_sum = jnp.sum(s_re * r_im - s_im * r_re, axis=1, keepdims=True)
    squares = jnp.sum(s_re * s_re + s_im * s_im, axis=1, keepdims=True)
    lane = lax.broadcasted_iota(jnp.int32, (F, 128), 1)
    mine = jnp.where(
        lane == 0, real_sum, jnp.where(lane == 1, imag_sum, jnp.where(lane == 2, squares, 0.0))
    )
    sums_send[...] = mine
    sums[member] = mine
    for device in mate_places:
        send_to(sums_send, sums.at[member], sums_send_sem, sums_recv_sem, device)

    for halo in halos:
        halo.wait_send()
    if groups > 1:
        wait_bytes(gathered.at[0], groups - 1, wide_send_sem)
        wait_bytes(group_multipoles, groups - 1, across_send_sem)
    wait_bytes(gathered, GROUP - 1, gather_send_sem)
    wait_bytes(contributions, GROUP - 1, up_send_sem)
    wait_bytes(group_locals, GROUP - 1, down_send_sem)

    wait_bytes(sums, GROUP - 1, sums_recv_sem)
    total = jnp.sum(sums[...], axis=0)
    totals_send[...] = total
    totals[group] = total
    for device in far_places:
        send_to(totals_send, totals.at[group], totals_send_sem, totals_recv_sem, device)
    wait_bytes(sums, GROUP - 1, sums_send_sem)
    if groups > 1:
        wait_bytes(totals, groups - 1, totals_recv_sem)
    total = jnp.sum(totals[...], axis=0).T
    rayleigh_ref[...] = total[0:2, :] / (total[2:3, :] + 1e-06)
    if groups > 1:
        wait_bytes(totals, groups - 1, totals_send_sem)


def on_device(
    sec_size,
    dev_size,
    sources,
    positions,
    weights,
    wavenumbers,
    directions,
    box_centers,
    group_centers,
    near_pairs,
    pair_counts,
    box_lists,
    group_lists,
):
    count = sec_size * dev_size
    groups = count // GROUP
    hbm = pl.BlockSpec(memory_space=pltpu.HBM)
    vmem = pl.BlockSpec(memory_space=pltpu.VMEM)
    f32 = jnp.float32
    result, rayleigh = pl.pallas_call(
        functools.partial(kernel, sec_size, dev_size, groups),
        out_shape=(
            jax.ShapeDtypeStruct((ROWS, P_DEV), f32),
            jax.ShapeDtypeStruct((2, F), f32),
        ),
        in_specs=[hbm] * 11,
        out_specs=(vmem, vmem),
        scratch_shapes=[
            pltpu.SMEM((F,), f32),
            pltpu.SMEM((3, count), f32),
            pltpu.SMEM((3, groups), f32),
            pltpu.SMEM((1, 2, PAIRS_MAX), jnp.int32),
            pltpu.SMEM((1,), jnp.int32),
            pltpu.SMEM((1, ML1), jnp.int32),
            pltpu.SMEM((ML2, groups), jnp.int32),
            pltpu.VMEM((ROWS, P_DEV), f32),
            pltpu.VMEM((3, P_DEV), f32),
            pltpu.VMEM((1, P_DEV), f32),
            pltpu.VMEM((3, Q), f32),
            pltpu.VMEM((2, LEAF, 128), f32),
            pltpu.VMEM((ROWS, 8, 128), f32),
            pltpu.VMEM((3, REC, P_DEV), f32),
            pltpu.VMEM((3 * LEAVES, LEAF, REC), f32),
            pltpu.VMEM((LEAVES, 8, LEAF), f32),
            pltpu.VMEM((1, Q, REC), f32),
            pltpu.VMEM((GROUP, groups, ROWS, Q), f32),
            pltpu.VMEM((F, 8, Q), f32),
            pltpu.VMEM((GROUP, 8, Q), f32),
            pltpu.VMEM((8, Q), f32),
            pltpu.VMEM((groups, 8, Q), f32),
            pltpu.VMEM((8, Q), f32),
            pltpu.VMEM((GROUP, 8, Q), f32),
            pltpu.VMEM((LEAVES, ROWS, 8, LEAF), f32),
            pltpu.VMEM((F, 128), f32),
            pltpu.VMEM((GROUP, F, 128), f32),
            pltpu.VMEM((F, 128), f32),
            pltpu.VMEM((groups, F, 128), f32),
            pltpu.SemaphoreType.DMA((11,)),
            pltpu.SemaphoreType.DMA((2,)),
            pltpu.SemaphoreType.DMA((2,)),
        ]
        + [pltpu.SemaphoreType.DMA] * 14,
        compiler_params=pltpu.CompilerParams(
            collective_id=0, has_side_effects=True, vmem_limit_bytes=32 * 1024 * 1024
        ),
        name="bem_matvec",
    )(
        wavenumbers,
        box_centers,
        group_centers,
        near_pairs,
        pair_counts,
        box_lists,
        group_lists.T,
        sources.reshape(ROWS, P_DEV),
        positions,
        weights[None, :],
        directions,
    )
    return result.reshape(2, F, P_DEV), rayleigh


def solution(mesh):
    in_specs = (
        P(None, None, ("sec", "dev")),
        P(None, ("sec", "dev")),
        P(("sec", "dev")),
        P(),
        P(),
        P(),
        P(),
        P(("sec", "dev"), None, None),
        P(("sec", "dev")),
        P(("sec", "dev"), None),
        P(),
    )
    out_specs = (P(None, None, ("sec", "dev")), P())
    return jax.shard_map(
        functools.partial(on_device, mesh.shape["sec"], mesh.shape["dev"]),
        mesh=mesh,
        in_specs=in_specs,
        out_specs=out_specs,
        check_vma=False,
    )
```

time: 36.6 us -> 38.4 us (1.049)
  local copies, waits for them, and re-layouts: 4.7 us -> 5.93 us
  Pallas kernels: 30.2 us -> 30.8 us
    unnamed x21 -> x22, local copies, waits for them, and re-layouts: 4.7 us -> 5.93 us
    pallas_call x1, Pallas kernels: 30.2 us -> 30.8 us  [on_device(): pl.pallas_call(functools.partial(kernel, sec_size, dev_size, groups), out...]
where the time goes in v2:
time: 38.4 us; the launch traced here: 38 us
  Pallas kernels  30.8 us (80%)
  local copies, waits for them, and re-layouts  5.93 us (15%)
  between operations  1.35 us (4%)
    pallas_call x1, Pallas kernels, on_device(): pl.pallas_call(functools.partial(kernel, sec_size, dev_size, groups), out...  30.8 us
    unnamed x22, local copies, waits for them, and re-layouts  5.93 us

profile of v2, /device:TPU:0, one launch (start us, length us, event | category | flops | bytes accessed | tf_op | source)
XLA Modules:
  0.0 38.0 jit_solution(2820252427381712086)
XLA Ops:
  0.6 0.0 copy-start.1
  1.3 0.0 copy-start.2
  1.3 0.0 copy-start.5
  1.3 0.0 copy-start.8
  1.3 0.0 copy-done.1
  1.3 0.6 %copy-done.2 = f32[3,32]{1,0:T(4,128)S(1)} copy-done((f32[3,32]{1,0:T(4,128)S(1)}, f32[3,32]{1,0:T(4,128)}, u32[]{:S(2)}) %copy-start.2) | copy-done | bytes 408
  2.0 0.0 copy-done.5
  2.0 0.0 copy-done.8
  2.0 0.0 copy-start
  2.0 0.7 %copy-done = f32[2,8,256]{2,1,0:T(8,128)S(1)} copy-done((f32[2,8,256]{2,1,0:T(8,128)S(1)}, f32[2,8,256]{2,1,0:T(8,128)}, u32[]{:S(2)}) %copy-start) | copy-done | bytes 16408
  2.7 0.0 copy-start.3
  2.7 0.7 %copy-done.3 = f32[3,4]{1,0:T(4,128)S(1)} copy-done((f32[3,4]{1,0:T(4,128)S(1)}, f32[3,4]{1,0:T(4,128)}, u32[]{:S(2)}) %copy-start.3) | copy-done | bytes 72
  3.4 0.0 copy-start.4
  3.4 0.7 %copy-done.4 = f32[3,128]{1,0:T(4,128)S(1)} copy-done((f32[3,128]{1,0:T(4,128)S(1)}, f32[3,128]{1,0:T(4,128)}, u32[]{:S(2)}) %copy-start.4) | copy-done | bytes 1560
  4.1 0.0 copy-start.6
  4.1 0.7 %copy-done.6 = s32[4,2]{0,1:T(2,128)S(1)} copy-done((s32[4,2]{0,1:T(2,128)S(1)}, s32[4,2]{0,1:T(2,128)}, u32[]{:S(2)}) %copy-start.6) | copy-done | bytes 56
  4.8 0.0 copy-start.7
  4.8 0.7 %copy-done.7 = f32[256]{0:T(256)S(1)} copy-done((f32[256]{0:T(256)S(1)}, f32[256]{0:T(256)}, u32[]{:S(2)}) %copy-start.7) | copy-done | bytes 1048
  5.4 0.0 copy-start.9
  5.4 0.7 %copy-done.9 = s32[1,4]{1,0:T(1,128)S(1)} copy-done((s32[1,4]{1,0:T(1,128)S(1)}, s32[1,4]{1,0:T(1,128)}, u32[]{:S(2)}) %copy-start.9) | copy-done | bytes 40
  6.1 30.8 %bem_matvec.1 = (f32[16,256]{1,0:T(8,128)S(1)}, f32[2,8]{1,0:T(2,128)S(1)}) custom-call(f32[8]{0:T(128)S(1)} %copy-done.8, f32[3,32]{1,0:T(4,128)S(1)} %copy-done.2, f32[3,4]{1,0:T(4,128)S(1)} %copy-done.3, s32[1,2,10]{2,1,0:T(2,128)S(1)} %copy-done.5, s32[1]{0:T(128)S(6)} %copy.15.counts_hbm, s32[1,4]{1,0:T(1,128)S(1)} %copy-done.9, s32[2,4]{1,0:T(2,128)S(1)} %bitcast.6, ...), custom_call_target="tpu_custom_call" | custom-call | tf_op jit(solution)/shard_map/bem_matvec/pallas_call | solution.py:491
  36.9 0.6 %copy.16 = f32[2,8,256]{2,1,0:T(8,128)} copy(f32[2,8,256]{2,1,0:T(8,128)S(1)} %bitcast.5) | data formatting | bytes 32768
  37.5 0.6 %copy.17 = f32[2,8]{1,0:T(2,128)} copy(f32[2,8]{1,0:T(2,128)S(1)} %get-tuple-element.9) | data formatting | bytes 128
Async XLA Ops:
  0.6 0.7 %copy-start.1 = (f32[3,256]{1,0:T(4,128)S(1)}, f32[3,256]{1,0:T(4,128)}, u32[]{:S(2)}) copy-start(f32[3,256]{1,0:T(4,128)} %positions_hbm.1) | copy-start | bytes 9220
  1.3 0.7 %copy-start.2 = (f32[3,32]{1,0:T(4,128)S(1)}, f32[3,32]{1,0:T(4,128)}, u32[]{:S(2)}) copy-start(f32[3,32]{1,0:T(4,128)} %centers_hbm.1) | copy-start | bytes 1156
  1.3 0.7 %copy-start.5 = (s32[1,2,10]{2,1,0:T(2,128)S(1)}, s32[1,2,10]{2,1,0:T(2,128)}, u32[]{:S(2)}) copy-start(s32[1,2,10]{2,1,0:T(2,128)} %pairs_hbm.1) | copy-start | bytes 244
  1.3 0.7 %copy-start.8 = (f32[8]{0:T(128)S(1)}, f32[8]{0:T(128)}, u32[]{:S(2)}) copy-start(f32[8]{0:T(128)} %wave_hbm.1) | copy-start | bytes 100
  2.0 0.7 %copy-start = (f32[2,8,256]{2,1,0:T(8,128)S(1)}, f32[2,8,256]{2,1,0:T(8,128)}, u32[]{:S(2)}) copy-start(f32[2,8,256]{2,1,0:T(8,128)} %param.11) | copy-start | bytes 49156
  2.7 0.7 %copy-start.3 = (f32[3,4]{1,0:T(4,128)S(1)}, f32[3,4]{1,0:T(4,128)}, u32[]{:S(2)}) copy-start(f32[3,4]{1,0:T(4,128)} %group_centers_hbm.1) | copy-start | bytes 148
  3.4 0.7 %copy-start.4 = (f32[3,128]{1,0:T(4,128)S(1)}, f32[3,128]{1,0:T(4,128)}, u32[]{:S(2)}) copy-start(f32[3,128]{1,0:T(4,128)} %directions_hbm.1) | copy-start | bytes 4612
  4.1 0.7 %copy-start.6 = (s32[4,2]{0,1:T(2,128)S(1)}, s32[4,2]{0,1:T(2,128)}, u32[]{:S(2)}) copy-start(s32[4,2]{0,1:T(2,128)} %param.21) | copy-start | bytes 100
  4.8 0.7 %copy-start.7 = (f32[256]{0:T(256)S(1)}, f32[256]{0:T(256)}, u32[]{:S(2)}) copy-start(f32[256]{0:T(256)} %param.13) | copy-start | bytes 3076
  5.4 0.7 %copy-start.9 = (s32[1,4]{1,0:T(1,128)S(1)}, s32[1,4]{1,0:T(1,128)}, u32[]{:S(2)}) copy-start(s32[1,4]{1,0:T(1,128)} %lists_hbm.1) | copy-start | bytes 52

commit v3 on v2

--- a/solution.py
+++ b/solution.py
@@ -24,6 +24,7 @@
 RADIUS_GROUP = 2.0 * RADIUS_BOX
 ROWS = 2 * F
 REC = 24
+SPLIT = 3 * ROWS
 BLOCK = 32
 ROUNDER = 12582912.0
 
@@ -55,7 +56,7 @@
 def geometry(target, cols):
     squared = SOFT * SOFT
     for axis in range(3):
-        offset = target[axis] - cols[:, ROWS + axis : ROWS + axis + 1]
+        offset = target[axis] - cols[:, axis : axis + 1]
         squared = squared + offset * offset
     inverse = lax.rsqrt(squared)
     distance = squared * inverse
@@ -76,27 +77,41 @@
     return block.reshape(block.shape[0] // 8, 8, block.shape[1]).sum(0)
 
 
-def apply_points(geo, target, load, turns, add):
+def apply_points(geo, spread, target, record, turns, add):
+    values, xyz = record
     blocks = range(LEAF // BLOCK)
     for block in blocks:
-        distance, inverse = geometry(target, load(block))
+        distance, inverse = geometry(target, xyz(block))
         geo[0, pl.ds(block * BLOCK, BLOCK), :] = distance
         geo[1, pl.ds(block * BLOCK, BLOCK), :] = inverse
     for f in range(F):
+        wide = jnp.dot(
+            values(), spread[:, f * 256 : (f + 1) * 256], preferred_element_type=jnp.float32
+        )
         total_re, total_im = 0.0, 0.0
         for block in blocks:
-            cols = load(block)
+            part = wide[block * BLOCK : (block + 1) * BLOCK]
             re, im = point_terms(
                 geo[0, pl.ds(block * BLOCK, BLOCK), :],
                 geo[1, pl.ds(block * BLOCK, BLOCK), :],
                 turns[f],
-                cols[:, f : f + 1],
-                cols[:, F + f : F + f + 1],
+                part[:, :128],
+                part[:, 128:],
             )
             total_re = total_re + fold(re)
             total_im = total_im + fold(im)
         add(f, total_re)
         add(F + f, total_im)
+
+
+def record_columns(rows):
+    values = rows[:ROWS]
+    high = values.astype(jnp.bfloat16).astype(jnp.float32)
+    rest = values - high
+    middle = rest.astype(jnp.bfloat16).astype(jnp.float32)
+    low = rest - middle
+    cols = jnp.concatenate([high, middle, low, rows[ROWS:]], axis=0).T
+    return cols[:, :SPLIT].astype(jnp.bfloat16), cols[:, SPLIT:]
 
 
 def adder(ref, first=False):
@@ -143,11 +158,14 @@
     weights_ref,
     directions_ref,
     geo,
+    spread,
     acc,
     window,
     records,
+    records_xyz,
     targets_xyz,
     scratch_rec,
+    scratch_xyz,
     gathered,
     contribution,
     contributions,
@@ -228,6 +246,10 @@
     partners = mate_places + far_places + [after, before]
     for partner in partners:
         pl.semaphore_signal(barrier, inc=1, device_id=partner, device_id_type=MESH)
+    row = lax.broadcasted_iota(jnp.int32, (SPLIT, 2 * 128 * F), 0) % ROWS
+    column = lax.broadcasted_iota(jnp.int32, (SPLIT, 2 * 128 * F), 1) // 128
+    spread[...] = jnp.where(row == column // 2 + F * (column % 2), 1.0, 0.0).astype(jnp.bfloat16)
+
     for operand in operands:
         operand.wait()
 
@@ -240,7 +262,7 @@
     window[1] = own_rows
     for leaf in range(LEAVES):
         part = own_rows[:, leaf * LEAF : (leaf + 1) * LEAF]
-        records[LEAVES + leaf] = part.T
+        records[LEAVES + leaf], records_xyz[LEAVES + leaf] = record_columns(part)
         targets_xyz[leaf] = part[ROWS : ROWS + 8]
     directions = directions_ref[...]
 
@@ -252,15 +274,21 @@
     row_padding = jnp.zeros((REC - ROWS - 3, Q), jnp.float32)
 
     def set_records(slot, rows, xyz):
-        scratch_rec[slot] = jnp.concatenate([rows, *xyz, row_padding], axis=0).T
+        scratch_rec[slot], scratch_xyz[slot] = record_columns(
+            jnp.concatenate([rows, *xyz, row_padding], axis=0)
+        )
 
     def loader(ref, index):
-        return lambda block: ref[index, pl.ds(pl.multiple_of(block * BLOCK, BLOCK), BLOCK), :]
+        xyz = records_xyz if ref is records else scratch_xyz
+        return (
+            lambda: ref[index],
+            lambda block: xyz[index, pl.ds(block * BLOCK, BLOCK), :],
+        )
 
     acc[...] = jnp.zeros_like(acc)
 
     def outward_leaf(leaf, carry):
-        apply_points(geo, own_proxies, loader(records, LEAVES + leaf), turns, adder(acc))
+        apply_points(geo, spread, own_proxies, loader(records, LEAVES + leaf), turns, adder(acc))
         return carry
 
     lax.fori_loop(0, LEAVES, outward_leaf, 0)
@@ -302,7 +330,7 @@
         send_to(own_slot, own_slot, wide_send_sem, wide_recv_sem, device)
 
     set_records(0, own_multipole, own_proxies)
-    apply_points(geo, parent_proxies, loader(scratch_rec, 0), turns, adder(acc, True))
+    apply_points(geo, spread, parent_proxies, loader(scratch_rec, 0), turns, adder(acc, True))
     terms = rows_of(acc[...]) * (RADIUS_GROUP / math.sqrt(GROUP * Q))
     padding = jnp.zeros((6, Q), jnp.float32)
     for f in range(F):
@@ -322,7 +350,10 @@
         rows = window[slot]
         rows = jnp.concatenate([rows[:ROWS] * inside, rows[ROWS:]], axis=0)
         for leaf in range(LEAVES):
-            records[slot * LEAVES + leaf] = rows[:, leaf * LEAF : (leaf + 1) * LEAF].T
+            index = slot * LEAVES + leaf
+            records[index], records_xyz[index] = record_columns(
+                rows[:, leaf * LEAF : (leaf + 1) * LEAF]
+            )
     near[...] = jnp.zeros_like(near)
 
     def near_pair(pair, carry):
@@ -337,7 +368,7 @@
                 near[leaf, row] += term * lives[leaf]
 
         apply_points(
-            geo, [xyz[axis : axis + 1] for axis in range(3)], loader(records, anchor), turns, add
+            geo, spread, [xyz[axis : axis + 1] for axis in range(3)], loader(records, anchor), turns, add
         )
         return carry
 
@@ -372,10 +403,10 @@
         other = group_lists_ref[m, group]
         rows = group_multipoles[other]
         xyz = proxies(group_centers_ref, other, RADIUS_GROUP)
-        cols = jnp.concatenate([rows, rows, *xyz, row_padding], axis=0).T
+        cols = jnp.concatenate([rows, *xyz, row_padding], axis=0).T
         for block in range(Q // BLOCK):
             part = cols[block * BLOCK : (block + 1) * BLOCK]
-            distance, inverse = geometry(parent_proxies, part)
+            distance, inverse = geometry(parent_proxies, part[:, 8:16])
             re, im = point_terms(distance, inverse, my_turns, part[:, 0:1], part[:, 1:2])
             local_re = local_re + fold(re)
             local_im = local_im + fold(im)
@@ -397,7 +428,7 @@
         set_records(
             0, gathered[other % GROUP, other // GROUP], proxies(centers_ref, other, RADIUS_BOX)
         )
-        apply_points(geo, own_proxies, loader(scratch_rec, 0), turns, adder(acc))
+        apply_points(geo, spread, own_proxies, loader(scratch_rec, 0), turns, adder(acc))
         return carry
 
     lax.fori_loop(0, ML1, list_box, 0)
@@ -408,7 +439,7 @@
         [group_locals[f][part : part + 1] for part in range(2) for f in range(F)], axis=0
     )
     set_records(0, rows, parent_proxies)
-    apply_points(geo, own_proxies, loader(scratch_rec, 0), turns, adder(acc, True))
+    apply_points(geo, spread, own_proxies, loader(scratch_rec, 0), turns, adder(acc, True))
     descended = rows_of(acc[...]) * (RADIUS_GROUP / math.sqrt(Q))
     set_records(0, incoming + descended, own_proxies)
 
@@ -421,7 +452,7 @@
             )
 
         apply_points(
-            geo, [xyz[axis : axis + 1] for axis in range(3)], loader(scratch_rec, 0), turns, add
+            geo, spread, [xyz[axis : axis + 1] for axis in range(3)], loader(scratch_rec, 0), turns, add
         )
         return carry
 
@@ -509,11 +540,14 @@
             pltpu.VMEM((1, P_DEV), f32),
             pltpu.VMEM((3, Q), f32),
             pltpu.VMEM((2, LEAF, 128), f32),
+            pltpu.VMEM((SPLIT, 2 * 128 * F), jnp.bfloat16),
             pltpu.VMEM((ROWS, 8, 128), f32),
             pltpu.VMEM((3, REC, P_DEV), f32),
-            pltpu.VMEM((3 * LEAVES, LEAF, REC), f32),
+            pltpu.VMEM((3 * LEAVES, LEAF, SPLIT), jnp.bfloat16),
+            pltpu.VMEM((3 * LEAVES, LEAF, REC - ROWS), f32),
             pltpu.VMEM((LEAVES, 8, LEAF), f32),
-            pltpu.VMEM((1, Q, REC), f32),
+            pltpu.VMEM((1, Q, SPLIT), jnp.bfloat16),
+            pltpu.VMEM((1, Q, REC - ROWS), f32),
             pltpu.VMEM((GROUP, groups, ROWS, Q), f32),
             pltpu.VMEM((F, 8, Q), f32),
             pltpu.VMEM((GROUP, 8, Q), f32),
@@ -532,7 +566,7 @@
         ]
         + [pltpu.SemaphoreType.DMA] * 14,
         compiler_params=pltpu.CompilerParams(
-            collective_id=0, has_side_effects=True, vmem_limit_bytes=32 * 1024 * 1024
+            collective_id=0, has_side_effects=True, vmem_limit_bytes=63 * 1024 * 1024
         ),
         name="bem_matvec",
     )(

time: 38.4 us -> 35.7 us (0.930)
  local copies, waits for them, and re-layouts: 5.93 us -> 1.89 us
  Pallas kernels: 30.8 us -> 32.2 us
    unnamed x22 -> x4, local copies, waits for them, and re-layouts: 5.93 us -> 1.89 us
    pallas_call x1, Pallas kernels: 30.8 us -> 32.2 us  [on_device(): pl.pallas_call(functools.partial(kernel, sec_size, dev_size, groups), out...]
where the time goes in v3:
time: 35.7 us; the launch traced here: 35.4 us
  Pallas kernels  32.2 us (90%)
  local copies, waits for them, and re-layouts  1.89 us (5%)
  between operations  1.3 us (4%)
    pallas_call x1, Pallas kernels, on_device(): pl.pallas_call(functools.partial(kernel, sec_size, dev_size, groups), out...  32.2 us
    unnamed x4, local copies, waits for them, and re-layouts  1.89 us

profile of v3, /device:TPU:0, one launch (start us, length us, event | category | flops | bytes accessed | tf_op | source)
XLA Modules:
  0.0 35.4 jit_solution(3231297835669424872)
XLA Ops:
  1.3 32.2 %bem_matvec.1 = (f32[16,256]{1,0:T(8,128)}, f32[2,8]{1,0:T(2,128)}) custom-call(f32[8]{0:T(128)} %wave_hbm.1, f32[3,32]{1,0:T(4,128)} %centers_hbm.1, f32[3,4]{1,0:T(4,128)} %group_centers_hbm.1, s32[1,2,10]{2,1,0:T(2,128)} %pairs_hbm.1, s32[1]{0:T(128)S(6)} %copy.15.counts_hbm, s32[1,4]{1,0:T(1,128)} %lists_hbm.1, s32[2,4]{1,0:T(2,128)} %bitcast.6, ...), custom_call_target="tpu_custom_call" | custom-call | tf_op jit(solution)/shard_map/bem_matvec/pallas_call | solution.py:522
  33.5 0.0 copy-start
  33.5 1.3 %copy.16 = f32[2,8,256]{2,1,0:T(8,128)} copy(f32[2,8,256]{2,1,0:T(8,128)} %bitcast.5) | data formatting | bytes 32768
  34.9 0.0 copy-done
  34.9 0.6 %copy.17 = f32[2,8]{1,0:T(2,128)} copy(f32[2,8]{1,0:T(2,128)S(1)} %copy-done) | data formatting | bytes 128
Async XLA Ops:
  33.5 1.3 %copy-start = (f32[2,8]{1,0:T(2,128)S(1)}, f32[2,8]{1,0:T(2,128)}, u32[]{:S(2)}) copy-start(f32[2,8]{1,0:T(2,128)} %get-tuple-element.9) | copy-start | bytes 196

commit v4 on v3

--- a/solution.py
+++ b/solution.py
@@ -26,22 +26,20 @@
 REC = 24
 SPLIT = 3 * ROWS
 BLOCK = 32
+TOGETHER = 2
 ROUNDER = 12582912.0
 
 COS = (
-    0.9999992216144897,
-    -19.738982519159087,
-    64.9287266658944,
-    -85.27239730229532,
-    58.794039342441934,
-    -21.076782244925596,
+    1.4142040807221545,
+    -6.977642062283951,
+    5.715238417642026,
+    -1.728348665863032,
 )
 SIN = (
-    6.283055797987737,
-    -41.33121426662637,
-    81.36681462152343,
-    -74.47800045497374,
-    32.7813926131928,
+    4.442867902973949,
+    -7.30744341898344,
+    3.5947880563486,
+    -0.7843739717150924,
 )
 MESH = pl.DeviceIdType.MESH
 
@@ -68,8 +66,10 @@
     phase = distance * turns
     phase = phase - ((phase + ROUNDER) - ROUNDER)
     z = phase * phase
-    cosine = inverse * horner(COS, z)
-    sine = (inverse * phase) * horner(SIN, z)
+    half_sine = phase * horner(SIN, z)
+    scaled = inverse * half_sine
+    cosine = inverse - scaled * half_sine
+    sine = scaled * horner(COS, z)
     return cosine * real - sine * imag, cosine * imag + sine * real
 
 
@@ -84,24 +84,28 @@
         distance, inverse = geometry(target, xyz(block))
         geo[0, pl.ds(block * BLOCK, BLOCK), :] = distance
         geo[1, pl.ds(block * BLOCK, BLOCK), :] = inverse
-    for f in range(F):
-        wide = jnp.dot(
-            values(), spread[:, f * 256 : (f + 1) * 256], preferred_element_type=jnp.float32
-        )
-        total_re, total_im = 0.0, 0.0
-        for block in blocks:
-            part = wide[block * BLOCK : (block + 1) * BLOCK]
-            re, im = point_terms(
-                geo[0, pl.ds(block * BLOCK, BLOCK), :],
-                geo[1, pl.ds(block * BLOCK, BLOCK), :],
-                turns[f],
-                part[:, :128],
-                part[:, 128:],
-            )
-            total_re = total_re + fold(re)
-            total_im = total_im + fold(im)
-        add(f, total_re)
-        add(F + f, total_im)
+
+    def frequencies(step, carry):
+        for offset in range(TOGETHER):
+            f = step * TOGETHER + offset
+            wide = jnp.dot(values(), spread[f], preferred_element_type=jnp.float32)
+            total_re, total_im = 0.0, 0.0
+            for block in blocks:
+                part = wide[block * BLOCK : (block + 1) * BLOCK]
+                re, im = point_terms(
+                    geo[0, pl.ds(block * BLOCK, BLOCK), :],
+                    geo[1, pl.ds(block * BLOCK, BLOCK), :],
+                    turns(f),
+                    part[:, :128],
+                    part[:, 128:],
+                )
+                total_re = total_re + fold(re)
+                total_im = total_im + fold(im)
+            add(f, total_re)
+            add(F + f, total_im)
+        return carry
+
+    lax.fori_loop(0, F // TOGETHER, frequencies, 0)
 
 
 def record_columns(rows):
@@ -144,7 +148,7 @@
     positions_hbm,
     weights_hbm,
     directions_hbm,
-    result_ref,
+    fields_ref,
     rayleigh_ref,
     wave_ref,
     centers_ref,
@@ -246,14 +250,16 @@
     partners = mate_places + far_places + [after, before]
     for partner in partners:
         pl.semaphore_signal(barrier, inc=1, device_id=partner, device_id_type=MESH)
-    row = lax.broadcasted_iota(jnp.int32, (SPLIT, 2 * 128 * F), 0) % ROWS
-    column = lax.broadcasted_iota(jnp.int32, (SPLIT, 2 * 128 * F), 1) // 128
-    spread[...] = jnp.where(row == column // 2 + F * (column % 2), 1.0, 0.0).astype(jnp.bfloat16)
+    row = lax.broadcasted_iota(jnp.int32, (SPLIT, 256), 0) % ROWS
+    column = lax.broadcasted_iota(jnp.int32, (SPLIT, 256), 1) // 128
+    for f in range(F):
+        spread[f] = jnp.where(row == f + F * column, 1.0, 0.0).astype(jnp.bfloat16)
 
     for operand in operands:
         operand.wait()
 
-    turns = [wave_ref[f] * (0.5 / math.pi) for f in range(F)]
+    def turns(f):
+        return wave_ref[f] * (0.5 / math.pi)
 
     weighted = sources_ref[...] * weights_ref[...]
     own_rows = jnp.concatenate(
@@ -397,7 +403,7 @@
 
     if groups > 1:
         wait_bytes(group_multipoles, groups - 1, across_recv_sem)
-    my_turns = wave_ref[member] * (0.5 / math.pi)
+    my_turns = turns(member)
     local_re, local_im = 0.0, 0.0
     for m in range(ML2):
         other = group_lists_ref[m, group]
@@ -458,8 +464,9 @@
 
     lax.fori_loop(0, LEAVES, far_leaf, 0)
     sources = sources_ref[...]
-    result = 0.5 * sources + jnp.concatenate([rows_of(near[leaf]) for leaf in range(LEAVES)], axis=1)
-    result_ref[...] = result
+    fields = jnp.concatenate([rows_of(near[leaf]) for leaf in range(LEAVES)], axis=1)
+    fields_ref[...] = fields
+    result = 0.5 * sources + fields
 
     s_re, s_im = sources[:F], sources[F:]
     r_re, r_im = result[:F], result[F:]
@@ -519,7 +526,7 @@
     hbm = pl.BlockSpec(memory_space=pltpu.HBM)
     vmem = pl.BlockSpec(memory_space=pltpu.VMEM)
     f32 = jnp.float32
-    result, rayleigh = pl.pallas_call(
+    fields, rayleigh = pl.pallas_call(
         functools.partial(kernel, sec_size, dev_size, groups),
         out_shape=(
             jax.ShapeDtypeStruct((ROWS, P_DEV), f32),
@@ -540,7 +547,7 @@
             pltpu.VMEM((1, P_DEV), f32),
             pltpu.VMEM((3, Q), f32),
             pltpu.VMEM((2, LEAF, 128), f32),
-            pltpu.VMEM((SPLIT, 2 * 128 * F), jnp.bfloat16),
+            pltpu.VMEM((F, SPLIT, 256), jnp.bfloat16),
             pltpu.VMEM((ROWS, 8, 128), f32),
             pltpu.VMEM((3, REC, P_DEV), f32),
             pltpu.VMEM((3 * LEAVES, LEAF, SPLIT), jnp.bfloat16),
@@ -582,7 +589,7 @@
         weights[None, :],
         directions,
     )
-    return result.reshape(2, F, P_DEV), rayleigh
+    return 0.5 * sources + fields.reshape(2, F, P_DEV), rayleigh
 
 
 def solution(mesh):

time: 35.7 us -> 38.6 us (1.081)
  Pallas kernels: 32.2 us -> 35.1 us
  other arithmetic: 0 us -> 1.33 us
  local copies, waits for them, and re-layouts: 1.89 us -> 0.57 us
    pallas_call x1, Pallas kernels: 32.2 us -> 35.1 us  [on_device(): pl.pallas_call(functools.partial(kernel, sec_size, dev_size, groups), out...]
    add x0 -> x1, other arithmetic: none -> 1.33 us  [on_device(): return (0.5 * sources + fields.reshape(2, F, P_DEV), rayleigh)]
    unnamed x4 -> x5, local copies, waits for them, and re-layouts: 1.89 us -> 0.57 us
where the time goes in v4:
time: 38.6 us; the launch traced here: 38.3 us
  Pallas kernels  35.1 us (91%)
  other arithmetic  1.33 us (3%)
  between operations  1.31 us (3%)
  local copies, waits for them, and re-layouts  0.57 us (1%)
    pallas_call x1, Pallas kernels, on_device(): pl.pallas_call(functools.partial(kernel, sec_size, dev_size, groups), out...  35.1 us
    add x1, other arithmetic, on_device(): return (0.5 * sources + fields.reshape(2, F, P_DEV), rayleigh)  1.33 us

profile of v4, /device:TPU:0, one launch (start us, length us, event | category | flops | bytes accessed | tf_op | source)
XLA Modules:
  0.0 38.3 jit_solution(16198191670887583361)
XLA Ops:
  1.3 0.0 copy-start
  1.3 35.1 %bem_matvec.1 = (f32[16,256]{1,0:T(8,128)}, f32[2,8]{1,0:T(2,128)}) custom-call(f32[8]{0:T(128)} %wave_hbm.1, f32[3,32]{1,0:T(4,128)} %centers_hbm.1, f32[3,4]{1,0:T(4,128)} %group_centers_hbm.1, s32[1,2,10]{2,1,0:T(2,128)} %pairs_hbm.1, s32[1]{0:T(128)S(6)} %copy.14.counts_hbm, s32[1,4]{1,0:T(1,128)} %lists_hbm.1, s32[2,4]{1,0:T(2,128)} %bitcast.6, ...), custom_call_target="tpu_custom_call" | custom-call | tf_op jit(solution)/shard_map/bem_matvec/pallas_call | solution.py:529
  36.4 0.0 copy-done
  36.4 0.0 copy-start.1
  36.4 1.3 %bitcast_add_fusion = f32[2,8,256]{2,1,0:T(8,128)} fusion(f32[16,256]{1,0:T(8,128)} %get-tuple-element.4, f32[2,8,256]{2,1,0:T(8,128)S(1)} %copy-done), kind=kLoop, calls=%fused_computation | loop fusion | flops 8192 | bytes 49152 | tf_op jit(solution)/shard_map/add | solution.py:592
  37.8 0.0 copy-done.1
  37.8 0.6 %copy.15 = f32[2,8]{1,0:T(2,128)} copy(f32[2,8]{1,0:T(2,128)S(1)} %copy-done.1) | data formatting | bytes 128
Async XLA Ops:
  1.3 35.1 %copy-start = (f32[2,8,256]{2,1,0:T(8,128)S(1)}, f32[2,8,256]{2,1,0:T(8,128)}, u32[]{:S(2)}) copy-start(f32[2,8,256]{2,1,0:T(8,128)} %param.11) | copy-start | bytes 49156
  36.4 1.3 %copy-start.1 = (f32[2,8]{1,0:T(2,128)S(1)}, f32[2,8]{1,0:T(2,128)}, u32[]{:S(2)}) copy-start(f32[2,8]{1,0:T(2,128)} %get-tuple-element.9) | copy-start | bytes 196

commit v5 on v4

--- a/solution.py
+++ b/solution.py
@@ -26,7 +26,7 @@
 REC = 24
 SPLIT = 3 * ROWS
 BLOCK = 32
-TOGETHER = 2
+JOBS = 2
 ROUNDER = 12582912.0
 
 COS = (
@@ -77,25 +77,23 @@
     return block.reshape(block.shape[0] // 8, 8, block.shape[1]).sum(0)
 
 
-def apply_points(geo, spread, target, record, turns, add):
-    values, xyz = record
-    blocks = range(LEAF // BLOCK)
-    for block in blocks:
-        distance, inverse = geometry(target, xyz(block))
-        geo[0, pl.ds(block * BLOCK, BLOCK), :] = distance
-        geo[1, pl.ds(block * BLOCK, BLOCK), :] = inverse
-
-    def frequencies(step, carry):
-        for offset in range(TOGETHER):
-            f = step * TOGETHER + offset
+def apply_points(geo, spread, turns, jobs):
+    blocks = [pl.ds(start, BLOCK) for start in range(0, LEAF, BLOCK)]
+    for slot, (target, (_, xyz), _) in enumerate(jobs):
+        for block in blocks:
+            distance, inverse = geometry(target, xyz(block))
+            geo[2 * slot, block, :] = distance
+            geo[2 * slot + 1, block, :] = inverse
+    for f in range(F):
+        for slot, (_, (values, _), add) in enumerate(jobs):
             wide = jnp.dot(values(), spread[f], preferred_element_type=jnp.float32)
             total_re, total_im = 0.0, 0.0
             for block in blocks:
-                part = wide[block * BLOCK : (block + 1) * BLOCK]
+                part = wide[block.start : block.start + BLOCK]
                 re, im = point_terms(
-                    geo[0, pl.ds(block * BLOCK, BLOCK), :],
-                    geo[1, pl.ds(block * BLOCK, BLOCK), :],
-                    turns(f),
+                    geo[2 * slot, block, :],
+                    geo[2 * slot + 1, block, :],
+                    turns[f],
                     part[:, :128],
                     part[:, 128:],
                 )
@@ -103,9 +101,6 @@
                 total_im = total_im + fold(im)
             add(f, total_re)
             add(F + f, total_im)
-        return carry
-
-    lax.fori_loop(0, F // TOGETHER, frequencies, 0)
 
 
 def record_columns(rows):
@@ -258,8 +253,7 @@
     for operand in operands:
         operand.wait()
 
-    def turns(f):
-        return wave_ref[f] * (0.5 / math.pi)
+    turns = [wave_ref[f] * (0.5 / math.pi) for f in range(F)]
 
     weighted = sources_ref[...] * weights_ref[...]
     own_rows = jnp.concatenate(
@@ -288,16 +282,19 @@
         xyz = records_xyz if ref is records else scratch_xyz
         return (
             lambda: ref[index],
-            lambda block: xyz[index, pl.ds(block * BLOCK, BLOCK), :],
+            lambda block: xyz[index, block, :],
         )
 
     acc[...] = jnp.zeros_like(acc)
-
-    def outward_leaf(leaf, carry):
-        apply_points(geo, spread, own_proxies, loader(records, LEAVES + leaf), turns, adder(acc))
-        return carry
-
-    lax.fori_loop(0, LEAVES, outward_leaf, 0)
+    apply_points(
+        geo,
+        spread,
+        turns,
+        [
+            (own_proxies, loader(records, LEAVES + leaf), adder(acc))
+            for leaf in range(LEAVES)
+        ],
+    )
     own_multipole = rows_of(acc[...]) * (RADIUS_BOX / math.sqrt(P_DEV))
     gathered[member, group] = own_multipole
 
@@ -336,7 +333,9 @@
         send_to(own_slot, own_slot, wide_send_sem, wide_recv_sem, device)
 
     set_records(0, own_multipole, own_proxies)
-    apply_points(geo, spread, parent_proxies, loader(scratch_rec, 0), turns, adder(acc, True))
+    apply_points(
+        geo, spread, turns, [(parent_proxies, loader(scratch_rec, 0), adder(acc, True))]
+    )
     terms = rows_of(acc[...]) * (RADIUS_GROUP / math.sqrt(GROUP * Q))
     padding = jnp.zeros((6, Q), jnp.float32)
     for f in range(F):
@@ -362,7 +361,7 @@
             )
     near[...] = jnp.zeros_like(near)
 
-    def near_pair(pair, carry):
+    def near_job(pair):
         target = pairs_ref[0, 0, pair]
         anchor = pairs_ref[0, 1, pair]
         live = jnp.where(pair < counts_ref[0], 1.0, 0.0)
@@ -373,13 +372,17 @@
             for leaf in range(LEAVES):
                 near[leaf, row] += term * lives[leaf]
 
+        return [xyz[axis : axis + 1] for axis in range(3)], loader(records, anchor), add
+
+    def near_turn(turn, carry):
         apply_points(
-            geo, spread, [xyz[axis : axis + 1] for axis in range(3)], loader(records, anchor), turns, add
+            geo, spread, turns, [near_job(turn * JOBS + offset) for offset in range(JOBS)]
         )
         return carry
 
-    first_half = PAIRS_MAX // 2
-    lax.fori_loop(0, first_half, near_pair, 0)
+    near_turns = PAIRS_MAX // JOBS
+    first_half = (near_turns + 1) // 2
+    lax.fori_loop(0, first_half, near_turn, 0)
 
     wait_bytes(contributions, GROUP - 1, up_recv_sem)
     total = contributions[0]
@@ -399,11 +402,11 @@
     for device in mate_places:
         send_to(own_part, own_part, gather_send_sem, gather_recv_sem, device)
 
-    lax.fori_loop(first_half, PAIRS_MAX, near_pair, 0)
+    lax.fori_loop(first_half, near_turns, near_turn, 0)
 
     if groups > 1:
         wait_bytes(group_multipoles, groups - 1, across_recv_sem)
-    my_turns = turns(member)
+    my_turns = wave_ref[member] * (0.5 / math.pi)
     local_re, local_im = 0.0, 0.0
     for m in range(ML2):
         other = group_lists_ref[m, group]
@@ -429,15 +432,20 @@
     wait_bytes(gathered, GROUP - 1, gather_recv_sem)
     acc[...] = jnp.zeros_like(acc)
 
-    def list_box(m, carry):
-        other = lists_ref[0, m]
-        set_records(
-            0, gathered[other % GROUP, other // GROUP], proxies(centers_ref, other, RADIUS_BOX)
-        )
-        apply_points(geo, spread, own_proxies, loader(scratch_rec, 0), turns, adder(acc))
+    def list_boxes(turn, carry):
+        jobs = []
+        for slot in range(JOBS):
+            other = lists_ref[0, turn * JOBS + slot]
+            set_records(
+                slot,
+                gathered[other % GROUP, other // GROUP],
+                proxies(centers_ref, other, RADIUS_BOX),
+            )
+            jobs.append((own_proxies, loader(scratch_rec, slot), adder(acc)))
+        apply_points(geo, spread, turns, jobs)
         return carry
 
-    lax.fori_loop(0, ML1, list_box, 0)
+    lax.fori_loop(0, ML1 // JOBS, list_boxes, 0)
     incoming = rows_of(acc[...]) * (RADIUS_BOX / math.sqrt(ML1 * Q))
 
     wait_bytes(group_locals, GROUP - 1, down_recv_sem)
@@ -445,11 +453,11 @@
         [group_locals[f][part : part + 1] for part in range(2) for f in range(F)], axis=0
     )
     set_records(0, rows, parent_proxies)
-    apply_points(geo, spread, own_proxies, loader(scratch_rec, 0), turns, adder(acc, True))
+    apply_points(geo, spread, turns, [(own_proxies, loader(scratch_rec, 0), adder(acc, True))])
     descended = rows_of(acc[...]) * (RADIUS_GROUP / math.sqrt(Q))
     set_records(0, incoming + descended, own_proxies)
 
-    def far_leaf(leaf, carry):
+    def far_job(leaf):
         xyz = targets_xyz[leaf]
 
         def add(row, term):
@@ -457,12 +465,9 @@
                 RADIUS_BOX / math.sqrt(Q)
             )
 
-        apply_points(
-            geo, spread, [xyz[axis : axis + 1] for axis in range(3)], loader(scratch_rec, 0), turns, add
-        )
-        return carry
-
-    lax.fori_loop(0, LEAVES, far_leaf, 0)
+        return [xyz[axis : axis + 1] for axis in range(3)], loader(scratch_rec, 0), add
+
+    apply_points(geo, spread, turns, [far_job(leaf) for leaf in range(LEAVES)])
     sources = sources_ref[...]
     fields = jnp.concatenate([rows_of(near[leaf]) for leaf in range(LEAVES)], axis=1)
     fields_ref[...] = fields
@@ -546,15 +551,15 @@
             pltpu.VMEM((3, P_DEV), f32),
             pltpu.VMEM((1, P_DEV), f32),
             pltpu.VMEM((3, Q), f32),
-            pltpu.VMEM((2, LEAF, 128), f32),
+            pltpu.VMEM((2 * JOBS, LEAF, 128), f32),
             pltpu.VMEM((F, SPLIT, 256), jnp.bfloat16),
             pltpu.VMEM((ROWS, 8, 128), f32),
             pltpu.VMEM((3, REC, P_DEV), f32),
             pltpu.VMEM((3 * LEAVES, LEAF, SPLIT), jnp.bfloat16),
             pltpu.VMEM((3 * LEAVES, LEAF, REC - ROWS), f32),
             pltpu.VMEM((LEAVES, 8, LEAF), f32),
-            pltpu.VMEM((1, Q, SPLIT), jnp.bfloat16),
-            pltpu.VMEM((1, Q, REC - ROWS), f32),
+            pltpu.VMEM((JOBS, Q, SPLIT), jnp.bfloat16),
+            pltpu.VMEM((JOBS, Q, REC - ROWS), f32),
             pltpu.VMEM((GROUP, groups, ROWS, Q), f32),
             pltpu.VMEM((F, 8, Q), f32),
             pltpu.VMEM((GROUP, 8, Q), f32),

time: 38.6 us -> 34.9 us (0.904)
  Pallas kernels: 35.1 us -> 31.5 us
    pallas_call x1, Pallas kernels: 35.1 us -> 31.5 us  [on_device(): pl.pallas_call(functools.partial(kernel, sec_size, dev_size, groups), out...]
where the time goes in v5:
time: 34.9 us; the launch traced here: 34.7 us
  Pallas kernels  31.5 us (90%)
  other arithmetic  1.33 us (4%)
  between operations  1.31 us (4%)
  local copies, waits for them, and re-layouts  0.57 us (2%)
    pallas_call x1, Pallas kernels, on_device(): pl.pallas_call(functools.partial(kernel, sec_size, dev_size, groups), out...  31.5 us
    add x1, other arithmetic, on_device(): return (0.5 * sources + fields.reshape(2, F, P_DEV), rayleigh)  1.33 us

profile of v5, /device:TPU:0, one launch (start us, length us, event | category | flops | bytes accessed | tf_op | source)
XLA Modules:
  0.0 34.7 jit_solution(9714747328355808694)
XLA Ops:
  1.3 0.0 copy-start
  1.3 31.5 %bem_matvec.1 = (f32[16,256]{1,0:T(8,128)}, f32[2,8]{1,0:T(2,128)}) custom-call(f32[8]{0:T(128)} %wave_hbm.1, f32[3,32]{1,0:T(4,128)} %centers_hbm.1, f32[3,4]{1,0:T(4,128)} %group_centers_hbm.1, s32[1,2,10]{2,1,0:T(2,128)} %pairs_hbm.1, s32[1]{0:T(128)S(6)} %copy.14.counts_hbm, s32[1,4]{1,0:T(1,128)} %lists_hbm.1, s32[2,4]{1,0:T(2,128)} %bitcast.6, ...), custom_call_target="tpu_custom_call" | custom-call | tf_op jit(solution)/shard_map/bem_matvec/pallas_call | solution.py:534
  32.8 0.0 copy-done
  32.8 0.0 copy-start.1
  32.8 1.3 %bitcast_add_fusion = f32[2,8,256]{2,1,0:T(8,128)} fusion(f32[16,256]{1,0:T(8,128)} %get-tuple-element.4, f32[2,8,256]{2,1,0:T(8,128)S(1)} %copy-done), kind=kLoop, calls=%fused_computation | loop fusion | flops 8192 | bytes 49152 | tf_op jit(solution)/shard_map/add | solution.py:597
  34.1 0.0 copy-done.1
  34.1 0.6 %copy.15 = f32[2,8]{1,0:T(2,128)} copy(f32[2,8]{1,0:T(2,128)S(1)} %copy-done.1) | data formatting | bytes 128
Async XLA Ops:
  1.3 31.5 %copy-start = (f32[2,8,256]{2,1,0:T(8,128)S(1)}, f32[2,8,256]{2,1,0:T(8,128)}, u32[]{:S(2)}) copy-start(f32[2,8,256]{2,1,0:T(8,128)} %param.11) | copy-start | bytes 49156
  32.8 1.3 %copy-start.1 = (f32[2,8]{1,0:T(2,128)S(1)}, f32[2,8]{1,0:T(2,128)}, u32[]{:S(2)}) copy-start(f32[2,8]{1,0:T(2,128)} %get-tuple-element.9) | copy-start | bytes 196
